TPU v7x, 256 devices: a whole 4x4x8 slice. The times are simulated.
256 devices in a mesh: chan: 32 (over z, x_hi, core), tm: 8 (over y, x_lo).
Axes of the slice: x: 4 (x_hi: 2, x_lo: 2; x = x_hi * 2 + x_lo), y: 4, z: 8, core: 2. Of those that a mesh axis runs over, the one named last changes fastest.
Arguments:
- spectra: bfloat16 [2048, 32, 2048], P('chan', 'tm'), may hold values from -400 to 400
- positions: int32 [2048], replicated, may hold values from 0 to 3070, as said below
- source_order: int32 [32], replicated, may hold values from 0 to 31, each once
Outputs:
- correlations: float32 [128, 2048], P('chan')
Inputs may be any that keep to these rules, and one draw needn't show every extreme that they name: positions start at 0 and rise by 1 or 2 from each channel to the next; exactly (2047) // 2 of the rises are 2. `source_order`: each block appears once.
All inputs are finite; a program needn't handle non-finite values.
Results may differ from a plain program's by a relative error of at most 0.005.
Values may be sent and summed in bfloat16 or wider, within the bound.
A program may use at most 64 MiB of HBM per device.

v0:
```python
import jax
import jax.numpy as jnp
from jax import lax
from jax.sharding import PartitionSpec as P

SRC = 64
BIN_DEV = 4
STEPS = 2


water_level = 0.1
pair_eps = 1e-06
block_rows = 8


def broadcast(value, axis, source):
    kept = jnp.where(lax.axis_index(axis) == source, value, 0).astype(value.dtype)
    return lax.psum(kept, axis)


def lag_block(owned, freq, width, first_lag, amount):
    freq_ids = jnp.arange(freq, dtype=jnp.int32)
    shifts = first_lag + jnp.arange(amount, dtype=jnp.int32) - freq
    phase = freq_ids[:, None] * shifts[None, :] % width
    angle = 2.0 * jnp.pi / width * phase.astype(jnp.float32)
    lagged = jnp.dot(owned[:, :freq], jnp.cos(angle), precision=lax.Precision.HIGHEST)
    return lagged - jnp.dot(owned[:, freq:], jnp.sin(angle), precision=lax.Precision.HIGHEST)


def local(spectra, positions, source_order):
    count_rows, seg_dev, width = spectra.shape
    freq = width // 2
    n_chan = lax.axis_size("chan")
    n_tm = lax.axis_size("tm")
    segs = seg_dev * n_tm
    data = spectra.astype(jnp.float32)
    power = jnp.sum(data[..., :freq] ** 2 + data[..., freq:] ** 2, axis=1)
    total = lax.psum(power, "tm")
    inverse = 1.0 / jnp.sqrt(total / segs + water_level)
    white = (data * jnp.concatenate([inverse, inverse], 1)[:, None, :]).astype(jnp.bfloat16)
    mine = lax.axis_index("chan")
    first = mine * count_rows
    channels = n_chan * count_rows
    bins = BIN_DEV * n_chan
    loop = channels + 1 + (channels - 1) // 2
    rec_pos = lax.dynamic_slice_in_dim(positions, first, count_rows, 0)
    rec_ids = first + jnp.arange(count_rows, dtype=jnp.int32)
    all_ids = jnp.arange(channels, dtype=jnp.int32)
    bin_iota = jnp.arange(bins, dtype=jnp.int32)[:, None]
    own_bins = mine * BIN_DEV + jnp.arange(BIN_DEV, dtype=jnp.int32)

    def offset_bins(left, right):
        gap = jnp.abs(left[:, None] - right[None, :])
        return jnp.minimum(gap, loop - gap) * (2 * bins) // (loop + 1)

    stack = jnp.zeros((bins, width), jnp.float32)
    counts = jnp.zeros((BIN_DEV,), jnp.float32)
    for step in range(STEPS):
        start = source_order[step] * SRC
        source = broadcast(white, "chan", start // count_rows)
        source_pos = lax.dynamic_slice_in_dim(positions, start, SRC, 0)

        def add_block(index, total):
            part = lax.dynamic_slice_in_dim(source, index * block_rows, block_rows, 0)
            part_pos = lax.dynamic_slice_in_dim(source_pos, index * block_rows, block_rows, 0)
            part_ids = start + index * block_rows + jnp.arange(block_rows, dtype=jnp.int32)
            real = jnp.zeros((block_rows, count_rows, freq), jnp.float32)
            imag = jnp.zeros((block_rows, count_rows, freq), jnp.float32)
            for segment in range(seg_dev):
                src_real = part[:, None, segment, :freq].astype(jnp.float32)
                src_imag = part[:, None, segment, freq:].astype(jnp.float32)
                rec_real = white[None, :, segment, :freq].astype(jnp.float32)
                rec_imag = white[None, :, segment, freq:].astype(jnp.float32)
                real = real + src_real * rec_real + src_imag * rec_imag
                imag = imag + src_real * rec_imag - src_imag * rec_real
            mean_square = (
                jnp.sum(real * real, axis=2, keepdims=True)
                + jnp.sum(imag * imag, axis=2, keepdims=True)
            ) / width
            scale = lax.rsqrt(mean_square + pair_eps)
            normed = jnp.concatenate(
                [(real * scale).astype(jnp.bfloat16), (imag * scale).astype(jnp.bfloat16)], 2
            )
            normed = normed.reshape(block_rows * count_rows, width)
            pair_bins = offset_bins(part_pos, rec_pos)
            valid = part_ids[:, None] != rec_ids[None, :]
            onehot = ((pair_bins.reshape(1, -1) == bin_iota) & valid.reshape(1, -1)).astype(
                jnp.bfloat16
            )
            return total + jnp.dot(onehot, normed, preferred_element_type=jnp.float32)

        stack = lax.fori_loop(0, SRC // block_rows, add_block, stack)
        every_bin = offset_bins(source_pos, positions)
        allowed = (start + jnp.arange(SRC, dtype=jnp.int32))[:, None] != all_ids[None, :]
        matched = (every_bin[:, :, None] == own_bins[None, None, :]) & allowed[:, :, None]
        counts = counts + jnp.sum(matched.astype(jnp.float32), axis=(0, 1))
    summed = lax.psum(stack, "tm")
    owned = lax.psum_scatter(summed, "chan", scatter_dimension=0, tiled=True)
    piece = min(512, width)
    lagged = jnp.concatenate(
        [lag_block(owned, freq, width, first_lag, piece) for first_lag in range(0, width, piece)], 1
    )
    return lagged / jnp.sqrt(counts * (n_tm * freq))[:, None]


def solution(mesh):
    return jax.shard_map(
        local,
        mesh=mesh,
        in_specs=(P("chan", "tm", None), P(), P()),
        out_specs=P("chan", None),
        check_vma=False,
    )
```

profile of v0, /device:TPU:1, one launch (start us, length us, event | category | flops | bytes accessed | tf_op | source)
XLA Modules:
  0.0 945.7 jit_solution(5194189302033040931)
XLA Ops:
  11.3 76.3 %all-reduce.6.cloned.1.call-done = f32[64,1024]{1,0:T(8,128)} async-done(((f32[64,1024]{1,0:T(8,128)}), f32[64,1024]{1,0:T(8,128)}) %all-reduce.6.cloned.1.call-update) | async-done | bytes 262160 | tf_op jit(solution)/shard_map/psum | solution.py:38
  92.0 278.7 %all-reduce.10.cloned.1.call-done = (bf16[64,4,2048]{2,0,1:T(8,128)(2,1)}, bf16[64,4,2048]{2,0,1:T(8,128)(2,1)}) async-done(((bf16[64,4,2048]{2,0,1:T(8,128)(2,1)}, bf16[64,4,2048]{2,0,1:T(8,128)(2,1)}), (bf16[64,4,2048]{2,0,1:T(8,128)(2,1)}, bf16[64,4,2048]{2,0,1:T(8,128)(2,1)})) %all-reduce.10.cloned.1.call-update) | async-done | bytes 2097168 | tf_op jit(solution)/shard_map/psum | solution.py:18
  370.7 100.1 %while.33 = (s32[]{:T(128)}, f32[128,2048]{1,0:T(8,128)}, s32[64]{0:T(128)S(1)}, s32[64]{0:T(128)S(1)}, s32[]{:T(128)}, /*index=5*/bf16[64,4,2048]{2,0,1:T(8,128...) while((s32[]{:T(128)}, f32[128,2048]{1,0:T(8,128)}, ...), condition=%wide.region_6.7_spmd.clone, body=%wide.region_3.6_spmd.clone.sunk | while | flops 293805632 | bytes 20610248 | solution.py:92
  371.8 4.1 multiply_reduce_fusion.7
  384.0 4.1 multiply_reduce_fusion.7
  396.6 4.1 multiply_reduce_fusion.7
  400.8 3.5 fusion.171
  409.1 4.1 multiply_reduce_fusion.7
  413.3 3.5 fusion.171
  421.7 4.1 multiply_reduce_fusion.7
  434.2 4.1 multiply_reduce_fusion.7
  446.8 4.1 multiply_reduce_fusion.7
  459.3 4.1 multiply_reduce_fusion.7
  470.8 100.1 %while.32 = (s32[]{:T(128)}, f32[128,2048]{1,0:T(8,128)}, s32[64]{0:T(128)S(1)}, s32[64]{0:T(128)S(1)}, s32[]{:T(128)}, /*index=5*/bf16[64,4,2048]{2,0,1:T(8,128...) while((s32[]{:T(128)}, f32[128,2048]{1,0:T(8,128)}, ...), condition=%wide.region_11.12_spmd.clone, body=%wide.region_8.11_spmd.clone.sunk | while | flops 293543488 | bytes 20610240 | solution.py:92
  471.9 4.1 multiply_reduce_fusion.6
  484.4 4.1 multiply_reduce_fusion.6
  496.9 4.1 multiply_reduce_fusion.6
  509.4 4.1 multiply_reduce_fusion.6
  521.9 4.1 multiply_reduce_fusion.6
  534.5 4.1 multiply_reduce_fusion.6
  547.0 4.1 multiply_reduce_fusion.6
  559.5 4.1 multiply_reduce_fusion.6
  574.2 266.2 %all-reduce.8.cloned.1.call-done = f32[128,2048]{1,0:T(8,128)} async-done(((f32[128,2048]{1,0:T(8,128)}), f32[128,2048]{1,0:T(8,128)}) %all-reduce.8.cloned.1.call-update) | async-done | bytes 1048592
  841.2 26.5 %psum.32 = f32[4,2048]{1,0:T(4,128)S(1)} all-reduce(f32[4,2048]{1,0:T(4,128)S(1)} %constant_dynamic-slice_fusion), channel_id=1, replica_groups=mesh['chan'=32,'tm'=8] {'tm'}, use_global_device_ids=true, to_apply=%region_12.13 | all-reduce | flops 8192 | bytes 65536 | tf_op jit(solution)/shard_map/psum | solution.py:97
  867.7 8.8 fusion.66
  876.5 8.8 fusion.78
  885.2 8.9 fusion.88
  894.1 8.8 fusion.72
  902.9 9.1 fusion.91
  912.0 8.7 fusion.94
  920.7 8.9 fusion.60
  929.6 8.7 fusion.97
  (259 shorter events, 138.5 us)
Async XLA Ops:
  6.5 81.0 %all-reduce.6.cloned.1.call-start = ((), (), s32[]{:S(2)}) async-start(), calls=%async_computation | async-start | bytes 524288 | tf_op jit(solution)/shard_map/psum | solution.py:38
  8.4 1.0 copy-start.2
  8.4 80.2 %copy-start = (bf16[64,4,2048]{2,1,0:T(4,128)(2,1)S(1)}, bf16[64,4,2048]{2,1,0:T(4,128)(2,1)}, u32[]{:S(2)}) copy-start(bf16[64,4,2048]{2,1,0:T(4,128)(2,1)} %param.7) | copy-start | bytes 3145732
  9.4 361.3 %all-reduce.10.cloned.1.call-start = ((), (), s32[]{:S(2)}) async-start(), calls=%async_computation.2 | async-start | bytes 4194304 | tf_op jit(solution)/shard_map/psum | solution.py:18
  90.3 1.2 copy-start.1
  91.5 748.9 %all-reduce.8.cloned.1.call-start = ((), (), s32[]{:S(2)}) async-start(), calls=%async_computation.1 | async-start | bytes 2097152
  470.8 100.2 %copy-start.3 = (u32[256]{0:T(256)S(1)}, u32[256]{0:T(256)}, u32[]{:S(2)}) copy-start(u32[256]{0:T(256)} %constant.319) | copy-start | bytes 3076
Sparse Core Ops, SparseCore 0:
  10.0 77.5 all-reduce.5
  91.6 279.0 all-reduce.9
  571.0 269.3 all-reduce.7
where the time goes:
time: 960 us; the launch traced here: 946 us
  waiting for transfers between devices  621 us (65%)
  other arithmetic  152 us (16%)
  matrix products  123 us (13%)
  blocking collectives  26.5 us (3%)
  between operations  15.4 us (2%)
    psum x1, waiting for transfers between devices, broadcast(): return lax.psum(kept, axis)  279 us
    unnamed x4, waiting for transfers between devices  266 us
    psum x1, waiting for transfers between devices, local(): total = lax.psum(power, 'tm')  76.3 us
    reduce_sum x16, other arithmetic, add_block(): jnp.sum(real * real, axis=2, keepdims=True)  66 us
    convert_element_type x16, other arithmetic, add_block(): (real * scale).astype(jnp.bfloat16)  55.8 us
    dot_general x16, matrix products, add_block(): return total + jnp.dot(onehot, normed, preferred_element_type=jnp.float32)  52.2 us
    dot_general x4, matrix products, lag_block(): jnp.dot(owned[:, :freq], jnp.cos(angle), precision=lax.Precision.HIGHEST)  35.4 us
    dot_general x4, matrix products, lag_block(): jnp.dot(owned[:, freq:], jnp.sin(angle), precision=lax.Precision.HIGHEST)  35.2 us
  transfers between devices with their start and end apart: 3, of which 3 were waited for; matrix products, arithmetic and copies ran while one was open for 0% of the time, Pallas kernels for 0%

commit v1 on v0

v1 whole, which is shorter than its diff:
```python
import functools

import jax
import jax.numpy as jnp
import numpy as np
from jax import lax
from jax.experimental import pallas as pl
from jax.experimental.pallas import tpu as pltpu
from jax.sharding import PartitionSpec as P

SRC = 64
STEPS = 2
SLOTS = 12
MIB = 1024 * 1024

water_level = 0.1
pair_eps = 1e-06
f32 = jnp.float32
bf16 = jnp.bfloat16


def to_bins(gap, loop, bins):
    offset = jnp.minimum(gap, loop - gap)
    return jnp.floor((offset * (2 * bins) + 0.5) * (1.0 / (loop + 1)))


def as_column(row):
    n = row.shape[1]
    eye = lax.broadcasted_iota(jnp.int32, (n, n), 0) == lax.broadcasted_iota(jnp.int32, (n, n), 1)
    return jnp.sum(jnp.where(eye, row, 0.0), axis=1, keepdims=True)


def corr_kernel(channels, bins, order_ref, pos_ref, w_ref, s_ref, out_ref,
                w2, s32, fs, fr, amat, hmask, wf0, wf1, t0, t1, acc):
    rows, width = w_ref.shape
    freq = width // 8
    loop = float(channels + 1 + (channels - 1) // 2)
    mine = lax.axis_index("chan")
    w2[:rows] = w_ref[...]
    w2[rows:] = w_ref[...]

    def unpack(i, _):
        r = pl.multiple_of(i * 16, 16)
        s32[pl.ds(r, 16), :] = s_ref[pl.ds(r, 16), :].astype(f32)
        return 0

    lax.fori_loop(0, STEPS * SRC // 16, unpack, 0)

    fw = fs.shape[1] // 16

    def features(x_ref, out, double, start, r):
        re = [x_ref[pl.ds(r, 16), pl.ds(pl.multiple_of(start + 2 * a * freq, fw), fw)].astype(f32)
              for a in range(4)]
        im = [x_ref[pl.ds(r, 16), pl.ds(pl.multiple_of(start + (2 * a + 1) * freq, fw), fw)].astype(f32)
              for a in range(4)]
        n = 0
        for a in range(4):
            out[pl.ds(r, 16), n * fw:(n + 1) * fw] = (re[a] * re[a] + im[a] * im[a]).astype(bf16)
            n += 1
        for a in range(4):
            for b in range(a + 1, 4):
                x = re[a] * re[b] + im[a] * im[b]
                y = re[a] * im[b] - im[a] * re[b]
                if double:
                    x, y = x + x, y + y
                out[pl.ds(r, 16), n * fw:(n + 1) * fw] = x.astype(bf16)
                out[pl.ds(r, 16), (n + 1) * fw:(n + 2) * fw] = y.astype(bf16)
                n += 2

    energy = jnp.zeros((STEPS * SRC, 2 * rows), f32)

    def add_energy(i, energy):
        start = pl.multiple_of(i * fw, fw)

        def one(j, _):
            r = pl.multiple_of(j * 16, 16)
            features(s_ref, fs, False, start, r)
            features(w2, fr, True, start, r)
            return 0

        lax.fori_loop(0, STEPS * SRC // 16, one, 0)
        return energy + lax.dot_general(fs[...], fr[...], (((1,), (1,)), ((), ())),
                                        preferred_element_type=f32)

    energy = lax.fori_loop(0, freq // fw, add_energy, energy)
    scale = lax.rsqrt(jnp.maximum(energy, 0.0) * (1.0 / (2 * freq)) + pair_eps)

    rec = pos_ref[pl.ds(mine, 1), :].astype(f32)
    lane = lax.broadcasted_iota(jnp.int32, (SRC, 2 * rows), 1)
    rec_ids = mine * rows + lane % rows
    firsts = []
    for step in range(STEPS):
        block = order_ref[step]
        src = as_column(pos_ref[pl.ds(block, 1), :].astype(f32)[:, :SRC])
        pair_bins = to_bins(jnp.abs(src - rec), loop, bins)
        src_ids = block * SRC + lax.broadcasted_iota(jnp.int32, (SRC, 2 * rows), 0)
        weight = jnp.where(src_ids == rec_ids, 0.0, scale[step * SRC:(step + 1) * SRC])
        first = jnp.min(jnp.min(pair_bins, axis=1, keepdims=True), axis=0, keepdims=True)
        firsts.append(first)
        rel = pair_bins - first
        upper = rel >= float(SLOTS)
        slot = jnp.where(upper, rel - float(SLOTS), rel)
        for k in range(SLOTS):
            here = slot == float(k)
            part = jnp.where(here, weight, 0.0)
            high = part.astype(bf16)
            low = (part - high.astype(f32)).astype(bf16)
            amat[step, k * SRC:(k + 1) * SRC, :] = jnp.where(lane < rows, high.astype(f32), low.astype(f32)).astype(bf16)
            mark = jnp.max(jnp.where(here & upper, 1.0, 0.0), axis=1, keepdims=True)
            hmask[step, k * SRC:(k + 1) * SRC, :] = jnp.broadcast_to(mark, (SRC, 128))

    chunks = freq // 128
    total = STEPS * chunks

    def project(i, wf, t):
        step, col = i // chunks, (i % chunks) * 128
        for n in range(8):
            wf[:, n * 128:(n + 1) * 128] = w2[:, pl.ds(pl.multiple_of(n * freq + col, 128), 128)]
        t[...] = jnp.dot(amat[step], wf[...], preferred_element_type=f32)

    def gather(i, t):
        step, col = i // chunks, pl.multiple_of((i % chunks) * 128, 128)
        for k in range(SLOTS):
            sums = [None] * 4
            for g in range(SRC // 8):
                r = k * SRC + g * 8
                row = pl.multiple_of(step * SRC + g * 8, 8)
                re, im = [], []
                for a in range(4):
                    tr = t[r:r + 8, 2 * a * 128:(2 * a + 1) * 128]
                    ti = t[r:r + 8, (2 * a + 1) * 128:(2 * a + 2) * 128]
                    sr = s32[pl.ds(row, 8), pl.ds(pl.multiple_of(2 * a * freq + col, 128), 128)]
                    si = s32[pl.ds(row, 8), pl.ds(pl.multiple_of((2 * a + 1) * freq + col, 128), 128)]
                    re += [sr * tr, si * ti]
                    im.append(sr * ti - si * tr)
                real = ((re[0] + re[1]) + (re[2] + re[3])) + ((re[4] + re[5]) + (re[6] + re[7]))
                imag = (im[0] + im[1]) + (im[2] + im[3])
                mark = hmask[step, r:r + 8, :]
                new = [real, imag, real * mark, imag * mark]
                sums = new if g == 0 else [x + y for x, y in zip(sums, new)]
            base = step * (2 * SLOTS * 8)
            acc[pl.ds(pl.multiple_of(base + k * 8, 8), 8), pl.ds(col, 128)] = sums[0]
            acc[pl.ds(pl.multiple_of(base + k * 8, 8), 8), pl.ds(pl.multiple_of(freq + col, 128), 128)] = sums[1]
            base = base + SLOTS * 8
            acc[pl.ds(pl.multiple_of(base + k * 8, 8), 8), pl.ds(col, 128)] = sums[2]
            acc[pl.ds(pl.multiple_of(base + k * 8, 8), 8), pl.ds(pl.multiple_of(freq + col, 128), 128)] = sums[3]

    project(0, wf0, t0)

    def pair(j, _):
        project(2 * j + 1, wf1, t1)
        gather(2 * j, t0)
        project(jnp.minimum(2 * j + 2, total - 1), wf0, t0)
        gather(2 * j + 1, t1)
        return 0

    lax.fori_loop(0, total // 2, pair, 0)

    span = 2 * SLOTS * 8
    col = lax.broadcasted_iota(jnp.int32, (bins, span), 1)
    row = lax.broadcasted_iota(jnp.int32, (bins, span), 0).astype(f32)
    marked = col >= SLOTS * 8
    k = ((col - jnp.where(marked, SLOTS * 8, 0)) // 8).astype(f32)
    place = []
    for step in range(STEPS):
        at = row == firsts[step] + k
        above = row == firsts[step] + k + float(SLOTS)
        place.append(jnp.where(marked, jnp.where(above, 1.0, 0.0) - jnp.where(at, 1.0, 0.0),
                               jnp.where(at, 1.0, 0.0)).astype(bf16))
    for c in range(0, width // 4, 256):
        out = jnp.zeros((bins, 256), f32)
        for step in range(STEPS):
            value = acc[step * span:(step + 1) * span, c:c + 256]
            high = value.astype(bf16)
            low = (value - high.astype(f32)).astype(bf16)
            out += jnp.dot(place[step], high, preferred_element_type=f32)
            out += jnp.dot(place[step], low, preferred_element_type=f32)
        out_ref[:, c:c + 256] = out


def correlate(white, sources, pos2, order, bins):
    rows, width = white.shape
    freq = width // 8
    sources_n = sources.shape[0]
    fw = 256
    vm = pl.BlockSpec(memory_space=pltpu.VMEM)
    return pl.pallas_call(
        functools.partial(corr_kernel, pos2.shape[0] * rows, bins),
        out_shape=jax.ShapeDtypeStruct((bins, 2 * freq), f32),
        in_specs=[pl.BlockSpec(memory_space=pltpu.SMEM), vm, vm, vm],
        out_specs=vm,
        scratch_shapes=[
            pltpu.VMEM((2 * rows, width), bf16),
            pltpu.VMEM((sources_n, width), f32),
            pltpu.VMEM((sources_n, 16 * fw), bf16),
            pltpu.VMEM((2 * rows, 16 * fw), bf16),
            pltpu.VMEM((STEPS, SLOTS * SRC, 2 * rows), bf16),
            pltpu.VMEM((STEPS, SLOTS * SRC, 128), f32),
            pltpu.VMEM((2 * rows, 1024), bf16),
            pltpu.VMEM((2 * rows, 1024), bf16),
            pltpu.VMEM((SLOTS * SRC, 1024), f32),
            pltpu.VMEM((SLOTS * SRC, 1024), f32),
            pltpu.VMEM((STEPS * 2 * SLOTS * 8, 2 * freq), f32),
        ],
        compiler_params=pltpu.CompilerParams(vmem_limit_bytes=56 * MIB),
        name="correlate",
    )(order, pos2, white, sources)


BIN_DEV = 4


def power_kernel(n_tm, x_ref, w_ref, part, got, inv, send1, recv1, send2, recv2):
    rows, width = x_ref.shape
    freq = width // 8
    cols = freq // n_tm
    me = lax.axis_index("tm")
    peers = [lax.rem(me + d, n_tm) for d in range(1, n_tm)]
    barrier = pltpu.get_barrier_semaphore()
    for peer in peers:
        pl.semaphore_signal(barrier, inc=1, device_id={"tm": peer})
    for p in range(n_tm):
        total = None
        for n in range(8):
            v = x_ref[:, n * freq + p * cols:n * freq + (p + 1) * cols].astype(f32)
            total = v * v if total is None else total + v * v
        part[p] = total.astype(bf16)
    pl.semaphore_wait(barrier, n_tm - 1)

    def exchange(src, dst, send, recv, d):
        return pltpu.make_async_remote_copy(src_ref=src, dst_ref=dst, send_sem=send, recv_sem=recv,
                                            device_id={"tm": peers[d - 1]})

    copies = [exchange(part.at[peers[d - 1]], got.at[me], send1.at[d], recv1.at[me], d) for d in range(1, n_tm)]
    for copy in copies:
        copy.start()
    total = part[me].astype(f32)
    for d in range(1, n_tm):
        other = lax.rem(me - d + n_tm, n_tm)
        exchange(part.at[me], got.at[other], send1.at[d], recv1.at[other], d).wait_recv()
        total = total + got[other].astype(f32)
    inv[me] = 1.0 / jnp.sqrt(total * (1.0 / (4 * n_tm)) + water_level)
    second = [exchange(inv.at[me], inv.at[me], send2.at[d], recv2.at[me], d) for d in range(1, n_tm)]
    for copy in second:
        copy.start()

    def whiten(p):
        factor = inv[p]
        for n in range(8):
            at = pl.ds(pl.multiple_of(n * freq + p * cols, cols), cols)
            w_ref[:, at] = (x_ref[:, at].astype(f32) * factor).astype(bf16)

    whiten(me)
    for d in range(1, n_tm):
        other = lax.rem(me - d + n_tm, n_tm)
        exchange(inv.at[me], inv.at[other], send2.at[d], recv2.at[other], d).wait_recv()
        whiten(other)
    for copy in copies + second:
        copy.wait_send()


def whiten(flat, n_tm):
    rows, width = flat.shape
    cols = width // 8 // n_tm
    vm = pl.BlockSpec(memory_space=pltpu.VMEM)
    return pl.pallas_call(
        functools.partial(power_kernel, n_tm),
        out_shape=jax.ShapeDtypeStruct((rows, width), bf16),
        in_specs=[vm],
        out_specs=vm,
        scratch_shapes=[
            pltpu.VMEM((n_tm, rows, cols), bf16),
            pltpu.VMEM((n_tm, rows, cols), bf16),
            pltpu.VMEM((n_tm, rows, cols), f32),
            pltpu.SemaphoreType.DMA((n_tm,)),
            pltpu.SemaphoreType.DMA((n_tm,)),
            pltpu.SemaphoreType.DMA((n_tm,)),
            pltpu.SemaphoreType.DMA((n_tm,)),
        ],
        compiler_params=pltpu.CompilerParams(collective_id=0, has_side_effects=True, vmem_limit_bytes=32 * MIB),
        name="whiten",
    )(flat)


def reduce_kernel(n_chan, n_tm, channels, bins, order_ref, pos_ref, stack_ref, table_ref, out_ref,
                  table, out0, got0, out1, got1, out2, got2, parts, xk,
                  table_sem, sem0, send1, recv1, send2, recv2, send3, recv3):
    width = stack_ref.shape[1]
    freq = width // 2
    loop = float(channels + 1 + (channels - 1) // 2)
    me_c, me_t = lax.axis_index("chan"), lax.axis_index("tm")
    zh, core = me_c // 2, lax.rem(me_c, 2)
    n_zh = n_chan // 2
    cols = freq // n_tm
    sibling = zh * 2 + 1 - core
    tms = [lax.rem(me_t + d, n_tm) for d in range(n_tm)]
    zhs = [lax.rem(zh + d, n_zh) for d in range(n_zh)]
    group = [(me_c, core, tms[d]) for d in range(1, n_tm)] + [(sibling, 1 - core, tms[d]) for d in range(n_tm)]
    back = [lax.rem(me_t - d + n_tm, n_tm) for d in range(n_tm)]
    group_back = [(core, back[d]) for d in range(1, n_tm)] + [(1 - core, back[d]) for d in range(n_tm)]
    barrier = pltpu.get_barrier_semaphore()
    for chan, _, tm in group:
        pl.semaphore_signal(barrier, inc=1, device_id={"chan": chan, "tm": tm})
    for q in zhs[1:]:
        pl.semaphore_signal(barrier, inc=1, device_id={"chan": q * 2 + core, "tm": me_t})
    load = pltpu.make_async_copy(table_ref, table, table_sem.at[0])
    load.start()

    def remote(src, dst, send, recv, chan, tm):
        return pltpu.make_async_remote_copy(src_ref=src, dst_ref=dst, send_sem=send, recv_sem=recv,
                                            device_id={"chan": chan, "tm": tm})

    out0[...] = stack_ref[:, pl.ds(pl.multiple_of((1 - core) * freq, freq), freq)].astype(bf16)
    pl.semaphore_wait(barrier, len(group) + n_zh - 1)
    swap = remote(out0, got0, sem0.at[0], sem0.at[1], sibling, me_t)
    swap.start()

    counts = []
    for step in range(STEPS):
        src = as_column(pos_ref[pl.ds(order_ref[step], 1), :].astype(f32)[:, :SRC])

        def count(i, sums):
            pair_bins = to_bins(jnp.abs(src - pos_ref[pl.ds(i, 1), :].astype(f32)), loop, bins)
            rel = pair_bins - (me_c * BIN_DEV).astype(f32)
            return tuple(s + jnp.where(rel == float(b), 0.5, 0.0) for b, s in enumerate(sums))

        init = tuple(jnp.zeros((SRC, pos_ref.shape[1]), f32) for _ in range(BIN_DEV))
        counts.append(lax.fori_loop(0, pos_ref.shape[0], count, init))
    factors = []
    for b in range(BIN_DEV):
        amount = sum(c[b] for c in counts)
        amount = jnp.sum(jnp.sum(amount, axis=1, keepdims=True), axis=0, keepdims=True)
        own = jnp.where(me_c * BIN_DEV + b == 0, float(STEPS * SRC), 0.0)
        factors.append(lax.rsqrt((amount - own) * float(n_tm * freq)))
    factor = jnp.concatenate(factors, 0)

    swap.wait()
    for p in range(n_tm):
        at = pl.ds(pl.multiple_of(core * freq + p * cols, cols), cols)
        out1[p] = (stack_ref[:, at] + got0[:, p * cols:(p + 1) * cols].astype(f32)).astype(bf16)
    first = [remote(out1.at[tms[d]], got1.at[me_t], send1.at[d], recv1.at[me_t], me_c, tms[d])
             for d in range(1, n_tm)]
    for copy in first:
        copy.start()
    total = out1[me_t].astype(f32)
    for d in range(1, n_tm):
        remote(out1.at[me_t], got1.at[back[d]], send1.at[d], recv1.at[back[d]], me_c, tms[d]).wait_recv()
        total = total + got1[back[d]].astype(f32)
    out2[...] = total.reshape(out2.shape)
    second = [remote(out2.at[zhs[d]], got2.at[zh], send2.at[d], recv2.at[zh], zhs[d] * 2 + core, me_t)
              for d in range(1, n_zh)]
    for copy in second:
        copy.start()
    total = out2[zh]
    for d in range(1, n_zh):
        other = lax.rem(zh - d + n_zh, n_zh)
        remote(out2.at[zh], got2.at[other], send2.at[d], recv2.at[other], zhs[d] * 2 + core, me_t).wait_recv()
        total = total + got2[other]
    slot = core * n_tm + me_t
    parts[slot] = total
    third = [remote(parts.at[slot], parts.at[slot], send3.at[i], recv3.at[slot], chan, tm)
             for i, (chan, _, tm) in enumerate(group)]
    for copy in third:
        copy.start()
    for i, ((chan, _, tm), (c, t)) in enumerate(zip(group, group_back)):
        other = c * n_tm + t
        remote(parts.at[slot], parts.at[other], send3.at[i], recv3.at[other], chan, tm).wait_recv()
    for n in range(2 * n_tm):
        value = parts[n]
        high = value.astype(bf16).astype(f32)
        xk[:, n * cols:(n + 1) * cols] = jnp.concatenate([high, value - high], 0).astype(bf16)
    load.wait()
    piece = 512
    for c in range(0, width, piece):
        both = jnp.dot(xk[...], table[:, c:c + piece], preferred_element_type=f32)
        both = both[:8] + both[8:]
        out_ref[:, c:c + piece] = jnp.where(core == 0, both[:BIN_DEV], both[BIN_DEV:]) * factor
    for copy in first + second + third:
        copy.wait_send()


def lag_table(freq):
    width = 2 * freq
    phase = np.outer(np.arange(freq), np.arange(width) - freq) % width
    angle = 2.0 * np.pi / width * phase
    return np.concatenate([np.cos(angle), -np.sin(angle)], 0).astype(jnp.bfloat16)


def reduce_stack(stack, pos2, order, n_chan, n_tm, channels):
    bins, width = stack.shape
    cols = width // 2 // n_tm
    n_zh = n_chan // 2
    vm = pl.BlockSpec(memory_space=pltpu.VMEM)
    dma = pltpu.SemaphoreType.DMA
    return pl.pallas_call(
        functools.partial(reduce_kernel, n_chan, n_tm, channels, bins),
        out_shape=jax.ShapeDtypeStruct((BIN_DEV, width), f32),
        in_specs=[pl.BlockSpec(memory_space=pltpu.SMEM), vm, vm, pl.BlockSpec(memory_space=pl.ANY)],
        out_specs=vm,
        scratch_shapes=[
            pltpu.VMEM((width, width), bf16),
            pltpu.VMEM((bins, width // 2), bf16),
            pltpu.VMEM((bins, width // 2), bf16),
            pltpu.VMEM((n_tm, bins, cols), bf16),
            pltpu.VMEM((n_tm, bins, cols), bf16),
            pltpu.VMEM((n_zh, bins // n_zh, cols), f32),
            pltpu.VMEM((n_zh, bins // n_zh, cols), f32),
            pltpu.VMEM((2 * n_tm, bins // n_zh, cols), f32),
            pltpu.VMEM((16, width), bf16),
            dma((1,)), dma((2,)), dma((n_tm,)), dma((n_tm,)), dma((n_zh,)), dma((n_zh,)),
            dma((2 * n_tm,)), dma((2 * n_tm,)),
        ],
        compiler_params=pltpu.CompilerParams(collective_id=1, has_side_effects=True, vmem_limit_bytes=48 * MIB),
        name="reduce_stack",
    )(order, pos2, stack, jnp.asarray(lag_table(width // 2)))


def local(spectra, positions, source_order):
    rows, seg_dev, width = spectra.shape
    n_chan = lax.axis_size("chan")
    n_tm = lax.axis_size("tm")
    bins = BIN_DEV * n_chan
    channels = n_chan * rows
    mine = lax.axis_index("chan")
    flat = spectra.reshape(rows, seg_dev * width)
    white = whiten(flat, n_tm)
    pos2 = positions.reshape(n_chan, rows)
    pos2 = jnp.concatenate([pos2, pos2], 1)
    sources = []
    for step in range(STEPS):
        kept = jnp.where(mine == source_order[step], white, 0).astype(bf16)
        sources.append(lax.psum(kept, "chan"))
    stack = correlate(white, jnp.concatenate(sources, 0), pos2, source_order, bins)
    return reduce_stack(stack, pos2, source_order, n_chan, n_tm, channels)


def solution(mesh):
    return jax.shard_map(
        local,
        mesh=mesh,
        in_specs=(P("chan", "tm", None), P(), P()),
        out_specs=P("chan", None),
        check_vma=False,
    )
```

time: 960 us -> 362 us (0.38); the launches traced: 946 us -> 362 us
  waiting for transfers between devices: 621 us -> 277 us
  other arithmetic: 152 us -> 5.38 us
  matrix products: 123 us -> 0 us
  Pallas kernels: 0 us -> 59.8 us
  blocking collectives: 26.5 us -> 0 us
    unnamed x4 -> x1, waiting for transfers between devices: 266 us -> 0.02 us
    dot_general x24 -> x0, matrix products: 123 us -> none  [the longest x16 52.2 us: add_block(): return total + jnp.dot(onehot, normed, preferred_element_type=jnp.float32)]
    psum x2 -> x1, waiting for transfers between devices: 355 us -> 277 us  [local(): sources.append(lax.psum(kept, 'chan'))]
    reduce_sum x18 -> x0, other arithmetic: 67.9 us -> none  [the longest x16 66 us: add_block(): jnp.sum(real * real, axis=2, keepdims=True)]
    convert_element_type x33 -> x0, other arithmetic: 61.6 us -> none  [the longest x16 55.8 us: add_block(): (real * scale).astype(jnp.bfloat16)]
    pallas_call x0 -> x3, Pallas kernels: none -> 59.8 us  [the longest x1 26.2 us: reduce_stack(): pl.pallas_call(functools.partial(reduce_kernel, n_chan, n_tm, channels, b...]
    psum x1 -> x0, blocking collectives: 26.5 us -> none  [local(): summed = lax.psum(stack, 'tm')]
    mul x16 -> x0, other arithmetic: 13.7 us -> none  [add_block(): real = real + src_real * rec_real + src_imag * rec_imag]
  transfers between devices with their start and end apart: 3 -> 1, of which waited for: 3 -> 1; matrix products, arithmetic and copies ran while one was open for 0% -> 0% of each run, Pallas kernels for 0% -> 0%
where the time goes in v1:
time: 362 us
  waiting for transfers between devices  277 us (77%)
  Pallas kernels  59.8 us (17%)
  between operations  14.7 us (4%)
  other arithmetic  5.38 us (1%)
  local copies, waits for them, and re-layouts  5.13 us (1%)
    psum x1, waiting for transfers between devices, local(): sources.append(lax.psum(kept, 'chan'))  277 us
    pallas_call x1, Pallas kernels, reduce_stack(): pl.pallas_call(functools.partial(reduce_kernel, n_chan, n_tm, channels, b...  26.2 us
    pallas_call x1, Pallas kernels, correlate(): pl.pallas_call(functools.partial(corr_kernel, pos2.shape[0] * rows, bins)...  21 us
    pallas_call x1, Pallas kernels, whiten(): pl.pallas_call(functools.partial(power_kernel, n_tm), out_shape=jax.Shape...  12.7 us
  transfers between devices with their start and end apart: 1, of which 1 were waited for; matrix products, arithmetic and copies ran while one was open for 0% of the time, Pallas kernels for 0%

profile of v1, /device:TPU:1, one launch (start us, length us, event | category | flops | bytes accessed | tf_op | source)
XLA Modules:
  0.0 362.0 jit_solution(7547840267214813336)
XLA Ops:
  6.5 0.0 all-reduce.3.cloned.1.call-start
  6.5 1.4 fusion
  9.2 1.8 copy.5
  11.0 0.0 copy-start.4
  11.0 12.7 %whiten.1.w_ref = bf16[64,8192]{1,0:T(8,128)(2,1)S(1)} custom-call(bf16[64,8192]{1,0:T(8,128)(2,1)S(1)} %bitcast.4), custom_call_target="tpu_custom_call" | custom-call | tf_op jit(solution)/shard_map/whiten/pallas_call | solution.py:266
  23.7 0.0 copy-start
  23.7 1.6 broadcast_select_fusion.1
  25.3 0.0 all-reduce.3.cloned.1.call-update
  25.3 0.0 copy-done.4
  25.3 0.1 reshape.6
  25.4 0.7 pad_add_fusion.pos_ref
  26.1 276.9 %all-reduce.3.cloned.1.call-done = (bf16[64,8192]{1,0:T(8,128)(2,1)}, bf16[64,8192]{1,0:T(8,128)(2,1)}) async-done(((bf16[64,8192]{1,0:T(8,128)(2,1)}, bf16[64,8192]{1,0:T(8,128)(2,1)}), (bf16[64,8192]{1,0:T(8,128)(2,1)}, bf16[64,8192]{1,0:T(8,128)(2,1)})) %all-reduce.3.cloned.1.call-update) | async-done | bytes 2097168 | tf_op jit(solution)/shard_map/psum | solution.py:432
  303.0 0.0 copy-start.2
  303.0 0.0 copy-start.3
  303.0 3.1 pad_maximum_fusion.s_ref
  306.1 0.0 copy-done
  306.1 21.0 %correlate.1.stack_ref = f32[128,2048]{1,0:T(8,128)} custom-call(s32[32]{0:T(128)} %order_ref.3, s32[32,128]{1,0:T(8,128)} %pad_add_fusion.pos_ref, bf16[64,8192]{1,0:T(8,128)(2,1)} %copy-done, bf16[128,8192]{1,0:T(8,128)(2,1)} %pad_maximum_fusion.s_ref), custom_call_target="tpu_custom_call" | custom-call | tf_op jit(solution)/shard_map/correlate/pallas_call | solution.py:187
  327.1 0.0 copy-done.2
  327.1 0.0 copy-done.3
  327.1 0.0 copy-start.1
  327.1 1.2 copy-done.1
  328.3 26.2 %reduce_stack.1 = f32[4,2048]{1,0:T(4,128)S(1)} custom-call(s32[32]{0:T(128)S(1)} %copy-done.3, s32[32,128]{1,0:T(8,128)S(1)} %copy-done.2, f32[128,2048]{1,0:T(8,128)S(1)} %copy-done.1, bf16[2048,2048]{1,0:T(8,128)(2,1)} %constant.11.clone.table_ref), custom_call_target="tpu_custom_call" | custom-call | tf_op jit(solution)/shard_map/reduce_stack/pallas_call | solution.py:395
  354.5 0.6 copy.9
Async XLA Ops:
  6.5 296.5 %all-reduce.3.cloned.1.call-start = ((), (), s32[]{:S(2)}) async-start(), calls=%async_computation | async-start | bytes 4194304 | tf_op jit(solution)/shard_map/psum | solution.py:432
  11.0 14.3 %copy-start.4 = (s32[2048]{0:T(1024)S(1)}, s32[2048]{0:T(1024)}, u32[]{:S(2)}) copy-start(s32[2048]{0:T(1024)} %param.5) | copy-start | bytes 24580
  23.7 282.4 %copy-start = (bf16[64,8192]{1,0:T(8,128)(2,1)}, bf16[64,8192]{1,0:T(8,128)(2,1)S(1)}, u32[]{:S(2)}) copy-start(bf16[64,8192]{1,0:T(8,128)(2,1)S(1)} %whiten.1.w_ref) | copy-start | bytes 3145732
  303.0 24.1 %copy-start.2 = (s32[32,128]{1,0:T(8,128)S(1)}, s32[32,128]{1,0:T(8,128)}, u32[]{:S(2)}) copy-start(s32[32,128]{1,0:T(8,128)} %pad_add_fusion.pos_ref) | copy-start | bytes 49156
  303.0 24.1 %copy-start.3 = (s32[32]{0:T(128)S(1)}, s32[32]{0:T(128)}, u32[]{:S(2)}) copy-start(s32[32]{0:T(128)} %order_ref.3) | copy-start | bytes 388
  327.1 1.2 copy-start.1
Sparse Core Ops, SparseCore 0:
  25.5 277.5 all-reduce.2

commit v2 on v1

--- a/solution.py
+++ b/solution.py
@@ -39,23 +39,11 @@
     w2[:rows] = w_ref[...]
     w2[rows:] = w_ref[...]
 
-    def unpack(i, _):
-        r = pl.multiple_of(i * 16, 16)
-        s32[pl.ds(r, 16), :] = s_ref[pl.ds(r, 16), :].astype(f32)
-        return 0
-
-    lax.fori_loop(0, STEPS * SRC // 16, unpack, 0)
-
-    fw = fs.shape[1] // 16
-
-    def features(x_ref, out, double, start, r):
-        re = [x_ref[pl.ds(r, 16), pl.ds(pl.multiple_of(start + 2 * a * freq, fw), fw)].astype(f32)
-              for a in range(4)]
-        im = [x_ref[pl.ds(r, 16), pl.ds(pl.multiple_of(start + (2 * a + 1) * freq, fw), fw)].astype(f32)
-              for a in range(4)]
+    def features(x, out, double, r):
+        re, im = x[0::2], x[1::2]
         n = 0
         for a in range(4):
-            out[pl.ds(r, 16), n * fw:(n + 1) * fw] = (re[a] * re[a] + im[a] * im[a]).astype(bf16)
+            out[pl.ds(r, 16), n * 128:(n + 1) * 128] = (re[a] * re[a] + im[a] * im[a]).astype(bf16)
             n += 1
         for a in range(4):
             for b in range(a + 1, 4):
@@ -63,26 +51,25 @@
                 y = re[a] * im[b] - im[a] * re[b]
                 if double:
                     x, y = x + x, y + y
-                out[pl.ds(r, 16), n * fw:(n + 1) * fw] = x.astype(bf16)
-                out[pl.ds(r, 16), (n + 1) * fw:(n + 2) * fw] = y.astype(bf16)
+                out[pl.ds(r, 16), n * 128:(n + 1) * 128] = x.astype(bf16)
+                out[pl.ds(r, 16), (n + 1) * 128:(n + 2) * 128] = y.astype(bf16)
                 n += 2
 
-    energy = jnp.zeros((STEPS * SRC, 2 * rows), f32)
-
     def add_energy(i, energy):
-        start = pl.multiple_of(i * fw, fw)
-
-        def one(j, _):
-            r = pl.multiple_of(j * 16, 16)
-            features(s_ref, fs, False, start, r)
-            features(w2, fr, True, start, r)
-            return 0
-
-        lax.fori_loop(0, STEPS * SRC // 16, one, 0)
+        for step in range(STEPS):
+            for q in range(4):
+                r = step * SRC + q * 16
+                x = [s_ref[q // 2, q % 2, i, step, n].astype(f32) for n in range(8)]
+                for n in range(8):
+                    s32[i, n, r:r + 16, :] = x[n]
+                features(x, fs, False, r)
+        for r in range(0, 2 * rows, 16):
+            x = [w2[r:r + 16, pl.ds(pl.multiple_of(n * freq + i * 128, 128), 128)].astype(f32) for n in range(8)]
+            features(x, fr, True, r)
         return energy + lax.dot_general(fs[...], fr[...], (((1,), (1,)), ((), ())),
                                         preferred_element_type=f32)
 
-    energy = lax.fori_loop(0, freq // fw, add_energy, energy)
+    energy = lax.fori_loop(0, freq // 128, add_energy, jnp.zeros((STEPS * SRC, 2 * rows), f32))
     scale = lax.rsqrt(jnp.maximum(energy, 0.0) * (1.0 / (2 * freq)) + pair_eps)
 
     rec = pos_ref[pl.ds(mine, 1), :].astype(f32)
@@ -129,8 +116,8 @@
                 for a in range(4):
                     tr = t[r:r + 8, 2 * a * 128:(2 * a + 1) * 128]
                     ti = t[r:r + 8, (2 * a + 1) * 128:(2 * a + 2) * 128]
-                    sr = s32[pl.ds(row, 8), pl.ds(pl.multiple_of(2 * a * freq + col, 128), 128)]
-                    si = s32[pl.ds(row, 8), pl.ds(pl.multiple_of((2 * a + 1) * freq + col, 128), 128)]
+                    sr = s32[i % chunks, 2 * a, pl.ds(row, 8), :]
+                    si = s32[i % chunks, 2 * a + 1, pl.ds(row, 8), :]
                     re += [sr * tr, si * ti]
                     im.append(sr * ti - si * tr)
                 real = ((re[0] + re[1]) + (re[2] + re[3])) + ((re[4] + re[5]) + (re[6] + re[7]))
@@ -181,8 +168,6 @@
 def correlate(white, sources, pos2, order, bins):
     rows, width = white.shape
     freq = width // 8
-    sources_n = sources.shape[0]
-    fw = 256
     vm = pl.BlockSpec(memory_space=pltpu.VMEM)
     return pl.pallas_call(
         functools.partial(corr_kernel, pos2.shape[0] * rows, bins),
@@ -191,9 +176,9 @@
         out_specs=vm,
         scratch_shapes=[
             pltpu.VMEM((2 * rows, width), bf16),
-            pltpu.VMEM((sources_n, width), f32),
-            pltpu.VMEM((sources_n, 16 * fw), bf16),
-            pltpu.VMEM((2 * rows, 16 * fw), bf16),
+            pltpu.VMEM((freq // 128, 8, STEPS * SRC, 128), f32),
+            pltpu.VMEM((STEPS * SRC, 16 * 128), bf16),
+            pltpu.VMEM((2 * rows, 16 * 128), bf16),
             pltpu.VMEM((STEPS, SLOTS * SRC, 2 * rows), bf16),
             pltpu.VMEM((STEPS, SLOTS * SRC, 128), f32),
             pltpu.VMEM((2 * rows, 1024), bf16),
@@ -210,38 +195,123 @@
 BIN_DEV = 4
 
 
-def power_kernel(n_tm, x_ref, w_ref, part, got, inv, send1, recv1, send2, recv2):
+def spread_kernel(n_chan, n_tm, order_ref, x_ref, w_ref, all_ref,
+                  sib, part, got, inv, relay, relayed, keep, cross, crossed, ppart, pgot,
+                  sib_sem, send1, recv1, send2, recv2, ring_send, ring_recv, cross_sem,
+                  send3, recv3, swap_sem, out_send, out_recv, pass_send, pass_recv):
     rows, width = x_ref.shape
     freq = width // 8
     cols = freq // n_tm
-    me = lax.axis_index("tm")
-    peers = [lax.rem(me + d, n_tm) for d in range(1, n_tm)]
+    half, quarter = rows // 2, rows // 4
+    me_c, me = lax.axis_index("chan"), lax.axis_index("tm")
+    n_z = n_chan // 4
+    z, hi, core = me_c // 4, lax.rem(me_c // 2, 2), lax.rem(me_c, 2)
+    up, down = lax.rem(z + 1, n_z), lax.rem(z + n_z - 1, n_z)
+
+    def chan(zz, hh, cc):
+        return zz * 4 + hh * 2 + cc
+
+    sibling, partner = chan(z, hi, 1 - core), chan(z, 1 - hi, core)
+    ways = [chan(up, hi, core), chan(down, hi, core)]
+    peers = [lax.rem(me + d, n_tm) for d in range(n_tm)]
+    back = [lax.rem(me - d + n_tm, n_tm) for d in range(n_tm)]
     barrier = pltpu.get_barrier_semaphore()
-    for peer in peers:
-        pl.semaphore_signal(barrier, inc=1, device_id={"tm": peer})
+    for d in range(1, n_tm):
+        pl.semaphore_signal(barrier, inc=1, device_id={"chan": me_c, "tm": peers[d]})
+    for other in [sibling, partner] + ways:
+        pl.semaphore_signal(barrier, inc=1, device_id={"chan": other, "tm": me})
+    pl.semaphore_wait(barrier, n_tm - 1 + 4)
+
+    def remote(src, dst, send, recv, other_chan, other_tm):
+        return pltpu.make_async_remote_copy(src_ref=src, dst_ref=dst, send_sem=send, recv_sem=recv,
+                                            device_id={"chan": other_chan, "tm": other_tm})
+
+    share = remote(x_ref.at[pl.ds(pl.multiple_of((1 - core) * half, half), half)], sib,
+                   sib_sem.at[0], sib_sem.at[1], sibling, me)
+    share.start()
     for p in range(n_tm):
         total = None
         for n in range(8):
             v = x_ref[:, n * freq + p * cols:n * freq + (p + 1) * cols].astype(f32)
             total = v * v if total is None else total + v * v
         part[p] = total.astype(bf16)
-    pl.semaphore_wait(barrier, n_tm - 1)
-
-    def exchange(src, dst, send, recv, d):
-        return pltpu.make_async_remote_copy(src_ref=src, dst_ref=dst, send_sem=send, recv_sem=recv,
-                                            device_id={"tm": peers[d - 1]})
-
-    copies = [exchange(part.at[peers[d - 1]], got.at[me], send1.at[d], recv1.at[me], d) for d in range(1, n_tm)]
-    for copy in copies:
+    first = [remote(part.at[peers[d]], got.at[me], send1.at[d], recv1.at[me], me_c, peers[d])
+             for d in range(1, n_tm)]
+    for copy in first:
         copy.start()
+    share.wait()
+
+    subs = ring_send.shape[2]
+    per = 8 // subs
+    blocks = [order_ref[k] for k in range(STEPS)]
+    here = [blocks[k] // 4 == z for k in range(STEPS)]
+    own_core = [lax.rem(blocks[k], 2) == core for k in range(STEPS)]
+    mine_at = pl.ds(pl.multiple_of(core * half, half), half)
+
+    def own(k, n, plane):
+        at = pl.ds(pl.multiple_of(n * freq + plane * 128, 128), 128)
+        return jnp.where(own_core[k], x_ref[mine_at, at], sib[:, at])
+
+    def hop(k, t, s):
+        n = pl.ds(s * per, per)
+        return remote(relay.at[k, t, n], relayed.at[k, t, n], ring_send.at[k, t, s], ring_recv.at[k, t, s], ways[k], me)
+
+    def ring_round(t, with_wait):
+        for s in range(subs):
+            for k in range(STEPS):
+                plane = lax.rem(z + n_z - 1 - t, n_z) if k == 0 else lax.rem(z + t + 1, n_z)
+                if with_wait:
+                    hop(k, t - 1, s).wait_recv()
+                for n in range(s * per, (s + 1) * per):
+                    value = own(k, n, plane)
+                    if with_wait:
+                        value = jnp.where(here[k], value, relayed[k, t - 1, n])
+                    relay[k, t, n] = value
+                hop(k, t, s).start()
+
+    ring_round(0, False)
+
+    def more(t, _):
+        ring_round(t, True)
+        return 0
+
+    middle = (n_z - 1) // 2 + 1
+    lax.fori_loop(1, middle, more, 0)
+
     total = part[me].astype(f32)
     for d in range(1, n_tm):
-        other = lax.rem(me - d + n_tm, n_tm)
-        exchange(part.at[me], got.at[other], send1.at[d], recv1.at[other], d).wait_recv()
-        total = total + got[other].astype(f32)
+        remote(part.at[me], got.at[back[d]], send1.at[d], recv1.at[back[d]], me_c, peers[d]).wait_recv()
+        total = total + got[back[d]].astype(f32)
     inv[me] = 1.0 / jnp.sqrt(total * (1.0 / (4 * n_tm)) + water_level)
-    second = [exchange(inv.at[me], inv.at[me], send2.at[d], recv2.at[me], d) for d in range(1, n_tm)]
+    second = [remote(inv.at[me], inv.at[me], send2.at[d], recv2.at[me], me_c, peers[d]) for d in range(1, n_tm)]
     for copy in second:
+        copy.start()
+
+    lax.fori_loop(middle, n_z - 1, more, 0)
+
+    hi_at = pl.ds(pl.multiple_of(hi * quarter, quarter), quarter)
+    low_at = pl.ds(pl.multiple_of((1 - hi) * quarter, quarter), quarter)
+    for k in range(STEPS):
+        for s in range(subs):
+            hop(k, n_z - 2, s).wait_recv()
+        for n in range(8):
+            keep[k, n] = jnp.where(here[k], own(k, n, z), relayed[k, n_z - 2, n])
+            cross[k, n] = keep[k, n, low_at, :]
+    swap = remote(cross, crossed, cross_sem.at[0], cross_sem.at[1], partner, me)
+    swap.start()
+    swap.wait()
+    raw = []
+    for k in range(STEPS):
+        from_here = lax.rem(blocks[k] // 2, 2) == hi
+        total = None
+        for n in range(8):
+            v = jnp.where(from_here, keep[k, n, hi_at, :], crossed[k, n])
+            keep[k, n, :quarter] = v
+            v = v.astype(f32)
+            total = v * v if total is None else total + v * v
+        ppart[k * quarter:(k + 1) * quarter] = total.astype(bf16)
+    third = [remote(ppart, pgot.at[me], send3.at[d], recv3.at[me], me_c, peers[d]) for d in range(1, n_tm)]
+    for copy in third:
         copy.start()
 
     def whiten(p):
@@ -252,34 +322,118 @@
 
     whiten(me)
     for d in range(1, n_tm):
-        other = lax.rem(me - d + n_tm, n_tm)
-        exchange(inv.at[me], inv.at[other], send2.at[d], recv2.at[other], d).wait_recv()
-        whiten(other)
-    for copy in copies + second:
+        remote(inv.at[me], inv.at[back[d]], send2.at[d], recv2.at[back[d]], me_c, peers[d]).wait_recv()
+        whiten(back[d])
+
+    total = ppart[...].astype(f32)
+    for d in range(1, n_tm):
+        remote(ppart, pgot.at[back[d]], send3.at[d], recv3.at[back[d]], me_c, peers[d]).wait_recv()
+        total = total + pgot[back[d]].astype(f32)
+    factor = 1.0 / jnp.sqrt(total * (1.0 / (4 * n_tm)) + water_level)
+    for k in range(STEPS):
+        for n in range(8):
+            all_ref[core, hi, z, k, n] = (keep[k, n, :quarter].astype(f32)
+                                          * factor[k * quarter:(k + 1) * quarter]).astype(bf16)
+
+    side = remote(all_ref.at[core, hi, z], all_ref.at[core, hi, z], swap_sem.at[0], swap_sem.at[1], partner, me)
+    side.start()
+    side.wait()
+
+    def send_on(w, t, s):
+        plane = lax.rem(z + n_z - t, n_z) if w == 0 else lax.rem(z + t, n_z)
+        ref = all_ref.at[core, w, plane, s // 2, pl.ds((s % 2) * 4, 4)]
+        return remote(ref, ref, out_send.at[w, t, s], out_recv.at[w, t, s], ways[w], me)
+
+    def came(w, t, s):
+        plane = lax.rem(z + n_z - t - 1, n_z) if w == 0 else lax.rem(z + t + 1, n_z)
+        ref = all_ref.at[core, w, plane, s // 2, pl.ds((s % 2) * 4, 4)]
+        return remote(ref, ref, out_send.at[w, t, s], out_recv.at[w, t, s], ways[w], me)
+
+    def pass_over(w, t):
+        plane = lax.rem(z + n_z - t, n_z) if w == 0 else lax.rem(z + t, n_z)
+        ref = all_ref.at[core, w, plane]
+        return remote(ref, ref, pass_send.at[w, t], pass_recv.at[w, t], sibling, me)
+
+    def passed(w, t):
+        plane = lax.rem(z + n_z - t, n_z) if w == 0 else lax.rem(z + t, n_z)
+        ref = all_ref.at[1 - core, w, plane]
+        return remote(ref, ref, pass_send.at[w, t], pass_recv.at[w, t], sibling, me)
+
+    for w in range(2):
+        for s in range(4):
+            send_on(w, 0, s).start()
+        pass_over(w, 0).start()
+
+    def onward(t, _):
+        for s in range(4):
+            for w in range(2):
+                came(w, t - 1, s).wait_recv()
+                send_on(w, t, s).start()
+        for w in range(2):
+            pass_over(w, t).start()
+        return 0
+
+    lax.fori_loop(1, n_z - 1, onward, 0)
+    for w in range(2):
+        for s in range(4):
+            came(w, n_z - 2, s).wait_recv()
+        pass_over(w, n_z - 1).start()
+
+    def finish(t, _):
+        for w in range(2):
+            passed(w, t).wait_recv()
+            pass_over(w, t).wait_send()
+        return 0
+
+    lax.fori_loop(0, n_z, finish, 0)
+
+    def sent(t, _):
+        for w in range(2):
+            for s in range(4):
+                send_on(w, t, s).wait_send()
+            for s in range(subs):
+                hop(w, t, s).wait_send()
+        return 0
+
+    lax.fori_loop(0, n_z - 1, sent, 0)
+    for copy in first + second + third:
         copy.wait_send()
 
 
-def whiten(flat, n_tm):
+def spread(flat, order, n_chan, n_tm):
     rows, width = flat.shape
     cols = width // 8 // n_tm
+    n_z = n_chan // 4
+    subs = 4
+    half, quarter = rows // 2, rows // 4
     vm = pl.BlockSpec(memory_space=pltpu.VMEM)
+    dma = pltpu.SemaphoreType.DMA
     return pl.pallas_call(
-        functools.partial(power_kernel, n_tm),
-        out_shape=jax.ShapeDtypeStruct((rows, width), bf16),
-        in_specs=[vm],
-        out_specs=vm,
+        functools.partial(spread_kernel, n_chan, n_tm),
+        out_shape=[jax.ShapeDtypeStruct((rows, width), bf16),
+                   jax.ShapeDtypeStruct((2, 2, n_z, STEPS, 8, quarter, 128), bf16)],
+        in_specs=[pl.BlockSpec(memory_space=pltpu.SMEM), vm],
+        out_specs=[vm, vm],
         scratch_shapes=[
+            pltpu.VMEM((half, width), bf16),
             pltpu.VMEM((n_tm, rows, cols), bf16),
             pltpu.VMEM((n_tm, rows, cols), bf16),
             pltpu.VMEM((n_tm, rows, cols), f32),
-            pltpu.SemaphoreType.DMA((n_tm,)),
-            pltpu.SemaphoreType.DMA((n_tm,)),
-            pltpu.SemaphoreType.DMA((n_tm,)),
-            pltpu.SemaphoreType.DMA((n_tm,)),
+            pltpu.VMEM((STEPS, n_z - 1, 8, half, 128), bf16),
+            pltpu.VMEM((STEPS, n_z - 1, 8, half, 128), bf16),
+            pltpu.VMEM((STEPS, 8, half, 128), bf16),
+            pltpu.VMEM((STEPS, 8, quarter, 128), bf16),
+            pltpu.VMEM((STEPS, 8, quarter, 128), bf16),
+            pltpu.VMEM((STEPS * quarter, 128), bf16),
+            pltpu.VMEM((n_tm, STEPS * quarter, 128), bf16),
+            dma((2,)), dma((n_tm,)), dma((n_tm,)), dma((n_tm,)), dma((n_tm,)),
+            dma((STEPS, n_z - 1, subs)), dma((STEPS, n_z - 1, subs)), dma((2,)),
+            dma((n_tm,)), dma((n_tm,)), dma((2,)),
+            dma((2, n_z - 1, 4)), dma((2, n_z - 1, 4)), dma((2, n_z)), dma((2, n_z)),
         ],
-        compiler_params=pltpu.CompilerParams(collective_id=0, has_side_effects=True, vmem_limit_bytes=32 * MIB),
-        name="whiten",
-    )(flat)
+        compiler_params=pltpu.CompilerParams(collective_id=0, has_side_effects=True, vmem_limit_bytes=48 * MIB),
+        name="spread",
+    )(order, flat)
 
 
 def reduce_kernel(n_chan, n_tm, channels, bins, order_ref, pos_ref, stack_ref, table_ref, out_ref,
@@ -421,16 +575,11 @@
     n_tm = lax.axis_size("tm")
     bins = BIN_DEV * n_chan
     channels = n_chan * rows
-    mine = lax.axis_index("chan")
     flat = spectra.reshape(rows, seg_dev * width)
-    white = whiten(flat, n_tm)
+    white, sources = spread(flat, source_order, n_chan, n_tm)
     pos2 = positions.reshape(n_chan, rows)
     pos2 = jnp.concatenate([pos2, pos2], 1)
-    sources = []
-    for step in range(STEPS):
-        kept = jnp.where(mine == source_order[step], white, 0).astype(bf16)
-        sources.append(lax.psum(kept, "chan"))
-    stack = correlate(white, jnp.concatenate(sources, 0), pos2, source_order, bins)
+    stack = correlate(white, sources, pos2, source_order, bins)
     return reduce_stack(stack, pos2, source_order, n_chan, n_tm, channels)
 
 

time: 362 us -> 130 us (0.36)
  waiting for transfers between devices: 277 us -> 0 us
  Pallas kernels: 59.8 us -> 120 us
  between operations: 14.7 us -> 0.04 us
  other arithmetic: 5.38 us -> 0.68 us
  local copies, waits for them, and re-layouts: 5.13 us -> 8.81 us
    psum x1 -> x0, waiting for transfers between devices: 277 us -> none  [local(): sources.append(lax.psum(kept, 'chan'))]
    pallas_call x1, Pallas kernels: 12.7 us -> 75.7 us  [spread(): pl.pallas_call(functools.partial(spread_kernel, n_chan, n_tm), out_shape=...]
    unnamed x12 -> x14, local copies, waits for them, and re-layouts: 3.7 us -> 8.05 us
  transfers between devices with their start and end apart: 1 -> 0, of which waited for: 1 -> 0; matrix products, arithmetic and copies ran while one was open for 0% -> 0% of each run, Pallas kernels for 0% -> 0%
where the time goes in v2:
time: 130 us
  Pallas kernels  120 us (92%)
  local copies, waits for them, and re-layouts  8.81 us (7%)
    pallas_call x1, Pallas kernels, spread(): pl.pallas_call(functools.partial(spread_kernel, n_chan, n_tm), out_shape=...  75.7 us
    pallas_call x1, Pallas kernels, reduce_stack(): pl.pallas_call(functools.partial(reduce_kernel, n_chan, n_tm, channels, b...  24.8 us
    pallas_call x1, Pallas kernels, correlate(): pl.pallas_call(functools.partial(corr_kernel, pos2.shape[0] * rows, bins)...  19.6 us
    unnamed x14, local copies, waits for them, and re-layouts  8.05 us

profile of v2, /device:TPU:1, one launch (start us, length us, event | category | flops | bytes accessed | tf_op | source)
XLA Modules:
  0.0 129.7 jit_solution(18373453997281698199)
XLA Ops:
  0.0 1.8 %copy.5 = bf16[8,8,4,2048]{3,1,2,0:T(8,128)(2,1)S(1)} copy(bf16[8,8,4,2048]{3,2,1,0:T(4,128)(2,1)} %bitcast.3) | data formatting | bytes 2097152
  1.8 0.0 copy-start.4
  1.9 0.6 copy-done.4
  2.5 75.7 %spread.1 = (bf16[64,8192]{1,0:T(8,128)(2,1)S(1)}, bf16[2,2,8,2,8,16,128]{6,5,4,3,2,1,0:T(8,128)(2,1)S(1)}) custom-call(s32[32]{0:T(128)S(1)} %copy-done.4, bf16[64,8192]{1,0:T(8,128)(2,1)S(1)} %bitcast.2), custom_call_target="tpu_custom_call" | custom-call | tf_op jit(solution)/shard_map/spread/pallas_call | solution.py:411
  78.2 0.0 copy-start.1
  78.2 1.3 %copy-done.1 = bf16[2,2,8,2,8,16,128]{6,5,4,3,2,1,0:T(8,128)(2,1)} copy-done((bf16[2,2,8,2,8,16,128]{6,5,4,3,2,1,0:T(8,128)(2,1)}, bf16[2,2,8,2,8,16,128]{6,5,4,3,2,1,0:T(8,128)(2,1)S(1)}, u32[]{:S(2)}) %copy-start.1) | copy-done | bytes 2097176
  79.6 0.0 copy-start.2
  79.6 1.0 copy-done.2
  80.6 0.8 reshape.6
  81.4 0.7 pad_add_fusion.pos_ref
  82.0 19.6 %correlate.1.stack_ref = f32[128,2048]{1,0:T(8,128)} custom-call(s32[32]{0:T(128)} %order_ref.5, s32[32,128]{1,0:T(8,128)} %pad_add_fusion.pos_ref, bf16[64,8192]{1,0:T(8,128)(2,1)} %copy-done.2, bf16[2,2,8,2,8,16,128]{6,5,4,3,2,1,0:T(8,128)(2,1)} %copy-done.1), custom_call_target="tpu_custom_call" | custom-call | tf_op jit(solution)/shard_map/correlate/pallas_call | solution.py:172
  101.7 0.0 copy-start
  101.7 1.2 copy-done
  102.9 0.0 copy-start.3
  102.9 0.7 copy-done.3
  103.6 0.0 copy-start.5
  103.6 0.7 copy-done.5
  104.3 24.8 %reduce_stack.1 = f32[4,2048]{1,0:T(4,128)S(1)} custom-call(s32[32]{0:T(128)S(1)} %copy-done.5, s32[32,128]{1,0:T(8,128)S(1)} %copy-done.3, f32[128,2048]{1,0:T(8,128)S(1)} %copy-done, bf16[2048,2048]{1,0:T(8,128)(2,1)} %constant.2.clone.table_ref), custom_call_target="tpu_custom_call" | custom-call | tf_op jit(solution)/shard_map/reduce_stack/pallas_call | solution.py:549
  129.1 0.6 copy.7
Async XLA Ops:
  1.8 0.7 copy-start.4
  78.2 1.4 %copy-start.1 = (bf16[2,2,8,2,8,16,128]{6,5,4,3,2,1,0:T(8,128)(2,1)}, bf16[2,2,8,2,8,16,128]{6,5,4,3,2,1,0:T(8,128)(2,1)S(1)}, u32[]{:S(2)}) copy-start(bf16[2,2,8,2,8,16,128]{6,5,4,3,2,1,0:T(8,128)(2,1)S(1)} %get-tuple-element.8.s_ref) | copy-start | bytes 6291460
  79.6 1.0 copy-start.2
  101.7 1.2 copy-start
  102.9 0.7 copy-start.3
  103.6 0.7 copy-start.5

commit v3 on v0

v3 whole, which is shorter than its diff:
```python
import functools

import jax
import jax.numpy as jnp
import numpy as np
from jax import lax
from jax.experimental import pallas as pl
from jax.experimental.pallas import tpu as pltpu
from jax.sharding import PartitionSpec as P

SRC = 64
STEPS = 2
SLOTS = 12
BIN_DEV = 4
MIB = 1024 * 1024

water_level = 0.1
pair_eps = 1e-06
f32 = jnp.float32
bf16 = jnp.bfloat16


def to_bins(gap, loop, bins):
    offset = jnp.minimum(gap, loop - gap)
    return jnp.floor((offset * (2 * bins) + 0.5) * (1.0 / (loop + 1)))


def as_column(row):
    n = row.shape[1]
    eye = lax.broadcasted_iota(jnp.int32, (n, n), 0) == lax.broadcasted_iota(jnp.int32, (n, n), 1)
    return jnp.sum(jnp.where(eye, row, 0.0), axis=1, keepdims=True)


def features(x, out, double):
    re, im = x[0::2], x[1::2]
    n = 0
    for a in range(4):
        out(n, re[a] * re[a] + im[a] * im[a])
        n += 1
    for a in range(4):
        for b in range(a + 1, 4):
            real = re[a] * re[b] + im[a] * im[b]
            imag = re[a] * im[b] - im[a] * re[b]
            if double:
                real, imag = real + real, imag + imag
            out(n, real)
            out(n + 1, imag)
            n += 2


def kernel(n_chan, n_tm, order_ref, pos_ref, x_ref, table_ref, out_ref,
           sib, part, got, inv, relay, relayed, keep, crossed, ppart, pgot, pieces,
           w2, s32, fs, fr, amat, hmask, wf0, wf1, t0, t1, acc,
           stack, table, out0, got0, out1, got1, out2, got2, owned, xk,
           table_sem, share_sem, send1, recv1, send2, recv2, ring_send, ring_recv, cross_sem,
           send3, recv3, around_send, around_recv, pass_send, pass_recv,
           swap_sem, send4, recv4, send5, recv5, send6, recv6):
    rows, width = x_ref.shape
    freq = width // 8
    cols = freq // n_tm
    half = rows // 2
    bins = BIN_DEV * n_chan
    channels = n_chan * rows
    loop = float(channels + 1 + (channels - 1) // 2)
    me_c, me = lax.axis_index("chan"), lax.axis_index("tm")
    n_z, n_zh = n_chan // 4, n_chan // 2
    zh, core = me_c // 2, lax.rem(me_c, 2)
    z, hi = zh // 2, lax.rem(zh, 2)
    sibling, partner = zh * 2 + 1 - core, z * 4 + (1 - hi) * 2 + core

    def above(d):
        return lax.rem(z + d + n_z, n_z)

    ways = [above(1) * 4 + hi * 2 + core, above(-1) * 4 + hi * 2 + core]
    reach = [n_z // 2, n_z - 1 - n_z // 2]
    tms = [lax.rem(me + d, n_tm) for d in range(n_tm)]
    back = [lax.rem(me - d + n_tm, n_tm) for d in range(n_tm)]
    zhs = [lax.rem(zh + d, n_zh) for d in range(n_zh)]
    group = [(me_c, core, tms[d]) for d in range(1, n_tm)] + [(sibling, 1 - core, tms[d]) for d in range(n_tm)]
    group_back = [(core, back[d]) for d in range(1, n_tm)] + [(1 - core, back[d]) for d in range(n_tm)]

    barrier = pltpu.get_barrier_semaphore()
    for chan, _, tm in group:
        pl.semaphore_signal(barrier, inc=1, device_id={"chan": chan, "tm": tm})
    for q in zhs[1:]:
        pl.semaphore_signal(barrier, inc=1, device_id={"chan": q * 2 + core, "tm": me})
    load = pltpu.make_async_copy(table_ref, table, table_sem.at[0])
    load.start()

    def remote(src, dst, send, recv, chan, tm):
        return pltpu.make_async_remote_copy(src_ref=src, dst_ref=dst, send_sem=send, recv_sem=recv,
                                            device_id={"chan": chan, "tm": tm})

    for p in range(n_tm):
        total = None
        for n in range(8):
            v = x_ref[:, n * freq + p * cols:n * freq + (p + 1) * cols].astype(f32)
            total = v * v if total is None else total + v * v
        part[p] = total.astype(bf16)
    pl.semaphore_wait(barrier, len(group) + n_zh - 1)

    share = remote(x_ref.at[pl.ds(pl.multiple_of((1 - core) * half, half), half)], sib,
                   share_sem.at[0], share_sem.at[1], sibling, me)
    share.start()
    first = [remote(part.at[tms[d]], got.at[me], send1.at[d], recv1.at[me], me_c, tms[d]) for d in range(1, n_tm)]
    for copy in first:
        copy.start()
    share.wait()

    blocks = [order_ref[k] for k in range(STEPS)]
    ahead = [lax.rem(z - blocks[k] // 4 + n_z, n_z) for k in range(STEPS)]
    own_core = [lax.rem(blocks[k], 2) == core for k in range(STEPS)]
    mine_at = pl.ds(pl.multiple_of(core * half, half), half)
    subs = [(k, s) for k in range(STEPS) for s in range(2)]

    def own(k, n, plane):
        at = pl.ds(pl.multiple_of(n * freq + plane * 128, 128), 128)
        return jnp.where(own_core[k], x_ref[mine_at, at], sib[:, at])

    def hop(w, t, k, s):
        n = pl.ds(s * 4, 4)
        return remote(relay.at[w, t, k, n], relayed.at[w, t, k, n], ring_send.at[w, t, 2 * k + s],
                      ring_recv.at[w, t, 2 * k + s], ways[w], me)

    def ring_round(t):
        for k, s in subs:
            for w in range(2):
                if t >= reach[w]:
                    continue
                plane = above(reach[w] - t) if w == 0 else above(t - reach[w])
                if t:
                    hop(w, t - 1, k, s).wait_recv()
                for n in range(s * 4, s * 4 + 4):
                    value = own(k, n, plane)
                    if t:
                        value = jnp.where(ahead[k] == 0, value, relayed[w, t - 1, k, n])
                    relay[w, t, k, n] = value
                hop(w, t, k, s).start()

    ring_round(0)

    counts = []
    for k in range(STEPS):
        src = as_column(pos_ref[pl.ds(blocks[k], 1), :].astype(f32)[:, :SRC])

        def count(i, sums):
            pair_bins = to_bins(jnp.abs(src - pos_ref[pl.ds(i, 1), :].astype(f32)), loop, bins)
            rel = pair_bins - (me_c * BIN_DEV).astype(f32)
            return tuple(s + jnp.where(rel == float(b), 0.5, 0.0) for b, s in enumerate(sums))

        init = tuple(jnp.zeros((SRC, pos_ref.shape[1]), f32) for _ in range(BIN_DEV))
        counts.append(lax.fori_loop(0, pos_ref.shape[0], count, init))
    factors = []
    for b in range(BIN_DEV):
        amount = sum(c[b] for c in counts)
        amount = jnp.sum(jnp.sum(amount, axis=1, keepdims=True), axis=0, keepdims=True)
        alone = jnp.where(me_c * BIN_DEV + b == 0, float(STEPS * SRC), 0.0)
        factors.append(lax.rsqrt((amount - alone) * float(n_tm * freq)))
    norm = jnp.concatenate(factors, 0)

    ring_round(1)

    total = part[me].astype(f32)
    for d in range(1, n_tm):
        remote(part.at[me], got.at[back[d]], send1.at[d], recv1.at[back[d]], me_c, tms[d]).wait_recv()
        total = total + got[back[d]].astype(f32)
    inv[me] = 1.0 / jnp.sqrt(total * (1.0 / (4 * n_tm)) + water_level)
    second = [remote(inv.at[me], inv.at[me], send2.at[d], recv2.at[me], me_c, tms[d]) for d in range(1, n_tm)]
    for copy in second:
        copy.start()

    for t in range(2, reach[0]):
        ring_round(t)

    for k, s in subs:
        for w in range(2):
            hop(w, reach[w] - 1, k, s).wait_recv()
        for n in range(s * 4, s * 4 + 4):
            value = jnp.where(ahead[k] <= reach[0], relayed[0, reach[0] - 1, k, n], relayed[1, reach[1] - 1, k, n])
            keep[k, n] = jnp.where(ahead[k] == 0, own(k, n, z), value)
    cross = remote(keep, crossed, cross_sem.at[0], cross_sem.at[1], partner, me)
    cross.start()

    def whiten(p):
        factor = inv[p]
        for n in range(8):
            at = pl.ds(pl.multiple_of(n * freq + p * cols, cols), cols)
            value = (x_ref[:, at].astype(f32) * factor).astype(bf16)
            w2[:rows, at] = value
            w2[rows:, at] = value

    whiten(me)
    for d in range(1, n_tm):
        remote(inv.at[me], inv.at[back[d]], send2.at[d], recv2.at[back[d]], me_c, tms[d]).wait_recv()
        whiten(back[d])

    cross.wait()
    for k in range(STEPS):
        from_here = lax.rem(blocks[k] // 2, 2) == hi
        total = None
        for n in range(8):
            value = jnp.where(from_here, keep[k, n], crossed[k, n])
            keep[k, n] = value
            value = value.astype(f32)
            total = value * value if total is None else total + value * value
        ppart[k * half:(k + 1) * half] = total.astype(bf16)
    third = [remote(ppart, pgot.at[me], send3.at[d], recv3.at[me], me_c, tms[d]) for d in range(1, n_tm)]
    for copy in third:
        copy.start()

    def receiver_features(i, _):
        for r in range(0, rows, 16):
            x = [w2[r:r + 16, pl.ds(pl.multiple_of(n * freq + i * 128, 128), 128)].astype(f32) for n in range(8)]

            def out(n, value):
                value = value.astype(bf16)
                fr[i, r:r + 16, n * 128:(n + 1) * 128] = value
                fr[i, rows + r:rows + r + 16, n * 128:(n + 1) * 128] = value

            features(x, out, True)
        return 0

    lax.fori_loop(0, n_z, receiver_features, 0)

    total = ppart[...].astype(f32)
    for d in range(1, n_tm):
        remote(ppart, pgot.at[back[d]], send3.at[d], recv3.at[back[d]], me_c, tms[d]).wait_recv()
        total = total + pgot[back[d]].astype(f32)
    factor = 1.0 / jnp.sqrt(total * (1.0 / (4 * n_tm)) + water_level)
    for k in range(STEPS):
        for n in range(8):
            pieces[core, z, k, n] = (keep[k, n].astype(f32) * factor[k * half:(k + 1) * half]).astype(bf16)

    def around(w, t, k, s, arriving):
        d = t + 1 if arriving else t
        ref = pieces.at[core, above(-d) if w == 0 else above(d), k, pl.ds(s * 4, 4)]
        return remote(ref, ref, around_send.at[w, t, 2 * k + s], around_recv.at[w, t, 2 * k + s], ways[w], me)

    def pass_over(d, c):
        ref = pieces.at[c, above(d)]
        slot = d + n_z // 2
        return remote(ref, ref, pass_send.at[slot], pass_recv.at[slot], sibling, me)

    def add_energy(d, energy):
        pass_over(d, 1 - core).wait_recv()
        plane = above(d)
        for k in range(STEPS):
            for q in range(4):
                r = k * SRC + q * 16
                x = [pieces[q // 2, plane, k, n, (q % 2) * 16:(q % 2) * 16 + 16, :].astype(f32) for n in range(8)]
                for n in range(8):
                    s32[plane, n, r:r + 16, :] = x[n]

                def out(n, value):
                    fs[r:r + 16, n * 128:(n + 1) * 128] = value.astype(bf16)

                features(x, out, False)
        return energy + lax.dot_general(fs[...], fr[plane], (((1,), (1,)), ((), ())), preferred_element_type=f32)

    for k, s in subs:
        for w in range(2):
            around(w, 0, k, s, False).start()
    pass_over(0, core).start()
    energy = jnp.zeros((STEPS * SRC, 2 * rows), f32)
    for t in range(1, reach[0] + 1):
        for k, s in subs:
            for w in range(2):
                if t <= reach[w]:
                    around(w, t - 1, k, s, True).wait_recv()
                if t < reach[w]:
                    around(w, t, k, s, False).start()
        pass_over(-t, core).start()
        if t <= reach[1]:
            pass_over(t, core).start()
        energy = add_energy(1 - t, energy)
        if t > 1 and t - 1 <= reach[1]:
            energy = add_energy(t - 1, energy)
    energy = add_energy(-reach[0], energy)
    scale = lax.rsqrt(jnp.maximum(energy, 0.0) * (1.0 / (2 * freq)) + pair_eps)

    rec = pos_ref[pl.ds(me_c, 1), :].astype(f32)
    lane = lax.broadcasted_iota(jnp.int32, (SRC, 2 * rows), 1)
    rec_ids = me_c * rows + lane % rows
    firsts = []
    for step in range(STEPS):
        block = blocks[step]
        src = as_column(pos_ref[pl.ds(block, 1), :].astype(f32)[:, :SRC])
        pair_bins = to_bins(jnp.abs(src - rec), loop, bins)
        src_ids = block * SRC + lax.broadcasted_iota(jnp.int32, (SRC, 2 * rows), 0)
        weight = jnp.where(src_ids == rec_ids, 0.0, scale[step * SRC:(step + 1) * SRC])
        lowest = jnp.min(jnp.min(pair_bins, axis=1, keepdims=True), axis=0, keepdims=True)
        firsts.append(lowest)
        rel = pair_bins - lowest
        upper = rel >= float(SLOTS)
        slot = jnp.where(upper, rel - float(SLOTS), rel)
        for k in range(SLOTS):
            here = slot == float(k)
            value = jnp.where(here, weight, 0.0)
            high = value.astype(bf16).astype(f32)
            amat[step, k * SRC:(k + 1) * SRC, :] = jnp.where(lane < rows, high, value - high).astype(bf16)
            mark = jnp.max(jnp.where(here & upper, 1.0, 0.0), axis=1, keepdims=True)
            hmask[step, k * SRC:(k + 1) * SRC, :] = jnp.broadcast_to(mark, (SRC, 128))

    chunks = freq // 128
    amount = STEPS * chunks

    def project(i, wf, t):
        step, col = i // chunks, (i % chunks) * 128
        for n in range(8):
            wf[:, n * 128:(n + 1) * 128] = w2[:, pl.ds(pl.multiple_of(n * freq + col, 128), 128)]
        t[...] = jnp.dot(amat[step], wf[...], preferred_element_type=f32)

    def gather(i, t):
        step, chunk = i // chunks, i % chunks
        col = pl.multiple_of(chunk * 128, 128)
        for k in range(SLOTS):
            sums = [None] * 4
            for g in range(SRC // 8):
                r = k * SRC + g * 8
                row = pl.multiple_of(step * SRC + g * 8, 8)
                re, im = [], []
                for a in range(4):
                    tr = t[r:r + 8, 2 * a * 128:(2 * a + 1) * 128]
                    ti = t[r:r + 8, (2 * a + 1) * 128:(2 * a + 2) * 128]
                    sr = s32[chunk, 2 * a, pl.ds(row, 8), :]
                    si = s32[chunk, 2 * a + 1, pl.ds(row, 8), :]
                    re += [sr * tr, si * ti]
                    im.append(sr * ti - si * tr)
                real = ((re[0] + re[1]) + (re[2] + re[3])) + ((re[4] + re[5]) + (re[6] + re[7]))
                imag = (im[0] + im[1]) + (im[2] + im[3])
                mark = hmask[step, r:r + 8, :]
                new = [real, imag, real * mark, imag * mark]
                sums = new if g == 0 else [x + y for x, y in zip(sums, new)]
            for part_n in range(2):
                base = pl.multiple_of(step * (2 * SLOTS * 8) + part_n * (SLOTS * 8) + k * 8, 8)
                acc[pl.ds(base, 8), pl.ds(col, 128)] = sums[2 * part_n]
                acc[pl.ds(base, 8), pl.ds(pl.multiple_of(freq + col, 128), 128)] = sums[2 * part_n + 1]

    project(0, wf0, t0)

    def pair(j, _):
        project(2 * j + 1, wf1, t1)
        gather(2 * j, t0)
        project(jnp.minimum(2 * j + 2, amount - 1), wf0, t0)
        gather(2 * j + 1, t1)
        return 0

    lax.fori_loop(0, amount // 2, pair, 0)

    span = 2 * SLOTS * 8
    col = lax.broadcasted_iota(jnp.int32, (bins, span), 1)
    row = lax.broadcasted_iota(jnp.int32, (bins, span), 0).astype(f32)
    marked = col >= SLOTS * 8
    k = ((col - jnp.where(marked, SLOTS * 8, 0)) // 8).astype(f32)
    place = []
    for step in range(STEPS):
        at = row == firsts[step] + k
        higher = row == firsts[step] + k + float(SLOTS)
        place.append(jnp.where(marked, jnp.where(higher, 1.0, 0.0) - jnp.where(at, 1.0, 0.0),
                               jnp.where(at, 1.0, 0.0)).astype(bf16))
    for c in range(0, 2 * freq, 256):
        out = jnp.zeros((bins, 256), f32)
        for step in range(STEPS):
            value = acc[step * span:(step + 1) * span, c:c + 256]
            high = value.astype(bf16)
            low = (value - high.astype(f32)).astype(bf16)
            out += jnp.dot(place[step], high, preferred_element_type=f32)
            out += jnp.dot(place[step], low, preferred_element_type=f32)
        stack[:, c:c + 256] = out

    out0[...] = stack[:, pl.ds(pl.multiple_of((1 - core) * freq, freq), freq)].astype(bf16)
    swap = remote(out0, got0, swap_sem.at[0], swap_sem.at[1], sibling, me)
    swap.start()
    swap.wait()
    for p in range(n_tm):
        at = pl.ds(pl.multiple_of(core * freq + p * cols, cols), cols)
        out1[p] = (stack[:, at] + got0[:, p * cols:(p + 1) * cols].astype(f32)).astype(bf16)
    fourth = [remote(out1.at[tms[d]], got1.at[me], send4.at[d], recv4.at[me], me_c, tms[d]) for d in range(1, n_tm)]
    for copy in fourth:
        copy.start()
    total = out1[me].astype(f32)
    for d in range(1, n_tm):
        remote(out1.at[me], got1.at[back[d]], send4.at[d], recv4.at[back[d]], me_c, tms[d]).wait_recv()
        total = total + got1[back[d]].astype(f32)
    out2[...] = total.reshape(out2.shape)
    fifth = [remote(out2.at[zhs[d]], got2.at[zh], send5.at[d], recv5.at[zh], zhs[d] * 2 + core, me)
             for d in range(1, n_zh)]
    for copy in fifth:
        copy.start()
    total = out2[zh]
    for d in range(1, n_zh):
        other = lax.rem(zh - d + n_zh, n_zh)
        remote(out2.at[zh], got2.at[other], send5.at[d], recv5.at[other], zhs[d] * 2 + core, me).wait_recv()
        total = total + got2[other]
    slot = core * n_tm + me
    owned[slot] = total
    sixth = [remote(owned.at[slot], owned.at[slot], send6.at[i], recv6.at[slot], chan, tm)
             for i, (chan, _, tm) in enumerate(group)]
    for copy in sixth:
        copy.start()
    for i, ((chan, _, tm), (c, t)) in enumerate(zip(group, group_back)):
        other = c * n_tm + t
        remote(owned.at[slot], owned.at[other], send6.at[i], recv6.at[other], chan, tm).wait_recv()
    for n in range(2 * n_tm):
        value = owned[n]
        high = value.astype(bf16).astype(f32)
        xk[:, n * cols:(n + 1) * cols] = jnp.concatenate([high, value - high], 0).astype(bf16)
    load.wait()
    piece = 512
    for c in range(0, 2 * freq, piece):
        both = jnp.dot(xk[...], table[:, c:c + piece], preferred_element_type=f32)
        both = both[:8] + both[8:]
        out_ref[:, c:c + piece] = jnp.where(core == 0, both[:BIN_DEV], both[BIN_DEV:]) * norm

    for w in range(2):
        for t in range(reach[w]):
            for k, s in subs:
                hop(w, t, k, s).wait_send()
                around(w, t, k, s, False).wait_send()
    for d in range(-reach[0], reach[1] + 1):
        pass_over(d, core).wait_send()
    for copy in first + second + third + fourth + fifth + sixth:
        copy.wait_send()


def lag_table(freq):
    width = 2 * freq
    phase = np.outer(np.arange(freq), np.arange(width) - freq) % width
    angle = 2.0 * np.pi / width * phase
    return np.concatenate([np.cos(angle), -np.sin(angle)], 0).astype(jnp.bfloat16)


def local(spectra, positions, source_order):
    rows, seg_dev, lags = spectra.shape
    n_chan = lax.axis_size("chan")
    n_tm = lax.axis_size("tm")
    bins = BIN_DEV * n_chan
    flat = spectra.reshape(rows, seg_dev * lags)
    pos2 = positions.reshape(n_chan, rows)
    pos2 = jnp.concatenate([pos2, pos2], 1)
    width = seg_dev * lags
    freq = lags // 2
    cols = freq // n_tm
    n_z, n_zh = n_chan // 4, n_chan // 2
    half = rows // 2
    up = n_z // 2
    vm = pl.BlockSpec(memory_space=pltpu.VMEM)
    dma = pltpu.SemaphoreType.DMA
    vmem = pltpu.VMEM
    return pl.pallas_call(
        functools.partial(kernel, n_chan, n_tm),
        out_shape=jax.ShapeDtypeStruct((BIN_DEV, lags), f32),
        in_specs=[pl.BlockSpec(memory_space=pltpu.SMEM), vm, vm, pl.BlockSpec(memory_space=pl.ANY)],
        out_specs=vm,
        scratch_shapes=[
            vmem((half, width), bf16),
            vmem((n_tm, rows, cols), bf16),
            vmem((n_tm, rows, cols), bf16),
            vmem((n_tm, rows, cols), f32),
            vmem((2, up, STEPS, 8, half, 128), bf16),
            vmem((2, up, STEPS, 8, half, 128), bf16),
            vmem((STEPS, 8, half, 128), bf16),
            vmem((STEPS, 8, half, 128), bf16),
            vmem((STEPS * half, 128), bf16),
            vmem((n_tm, STEPS * half, 128), bf16),
            vmem((2, n_z, STEPS, 8, half, 128), bf16),
            vmem((2 * rows, width), bf16),
            vmem((n_z, 8, STEPS * SRC, 128), f32),
            vmem((STEPS * SRC, 16 * 128), bf16),
            vmem((n_z, 2 * rows, 16 * 128), bf16),
            vmem((STEPS, SLOTS * SRC, 2 * rows), bf16),
            vmem((STEPS, SLOTS * SRC, 128), f32),
            vmem((2 * rows, 1024), bf16),
            vmem((2 * rows, 1024), bf16),
            vmem((SLOTS * SRC, 1024), f32),
            vmem((SLOTS * SRC, 1024), f32),
            vmem((STEPS * 2 * SLOTS * 8, lags), f32),
            vmem((bins, lags), f32),
            vmem((lags, lags), bf16),
            vmem((bins, freq), bf16),
            vmem((bins, freq), bf16),
            vmem((n_tm, bins, cols), bf16),
            vmem((n_tm, bins, cols), bf16),
            vmem((n_zh, bins // n_zh, cols), f32),
            vmem((n_zh, bins // n_zh, cols), f32),
            vmem((2 * n_tm, bins // n_zh, cols), f32),
            vmem((16, lags), bf16),
            dma((1,)), dma((2,)), dma((n_tm,)), dma((n_tm,)), dma((n_tm,)), dma((n_tm,)),
            dma((2, up, 4)), dma((2, up, 4)), dma((2,)), dma((n_tm,)), dma((n_tm,)),
            dma((2, up, 4)), dma((2, up, 4)), dma((n_z,)), dma((n_z,)),
            dma((2,)), dma((n_tm,)), dma((n_tm,)), dma((n_zh,)), dma((n_zh,)), dma((2 * n_tm,)), dma((2 * n_tm,)),
        ],
        compiler_params=pltpu.CompilerParams(collective_id=0, has_side_effects=True, vmem_limit_bytes=58 * MIB),
        name="offset_stack",
    )(source_order, pos2, flat, jnp.asarray(lag_table(freq)))


def solution(mesh):
    return jax.shard_map(
        local,
        mesh=mesh,
        in_specs=(P("chan", "tm", None), P(), P()),
        out_specs=P("chan", None),
        check_vma=False,
    )
```

time: 960 us -> 96 us (0.10); the launches traced: 946 us -> 95.7 us
  waiting for transfers between devices: 621 us -> 0 us
  other arithmetic: 152 us -> 0.68 us
  matrix products: 123 us -> 0 us
  Pallas kernels: 0 us -> 90.1 us
  blocking collectives: 26.5 us -> 0 us
  between operations: 15.4 us -> 0.01 us
    psum x2 -> x0, waiting for transfers between devices: 355 us -> none  [the longest x1 279 us: broadcast(): return lax.psum(kept, axis)]
    unnamed x4 -> x0, waiting for transfers between devices: 266 us -> none
    dot_general x24 -> x0, matrix products: 123 us -> none  [the longest x16 52.2 us: add_block(): return total + jnp.dot(onehot, normed, preferred_element_type=jnp.float32)]
    pallas_call x0 -> x1, Pallas kernels: none -> 90.1 us  [local(): pl.pallas_call(functools.partial(kernel, n_chan, n_tm), out_shape=jax.Sha...]
    reduce_sum x18 -> x0, other arithmetic: 67.9 us -> none  [the longest x16 66 us: add_block(): jnp.sum(real * real, axis=2, keepdims=True)]
    convert_element_type x33 -> x0, other arithmetic: 61.6 us -> none  [the longest x16 55.8 us: add_block(): (real * scale).astype(jnp.bfloat16)]
    psum x1 -> x0, blocking collectives: 26.5 us -> none  [local(): summed = lax.psum(stack, 'tm')]
    mul x16 -> x0, other arithmetic: 13.7 us -> none  [add_block(): real = real + src_real * rec_real + src_imag * rec_imag]
  transfers between devices with their start and end apart: 3 -> 0, of which waited for: 3 -> 0; matrix products, arithmetic and copies ran while one was open for 0% -> 0% of each run, Pallas kernels for 0% -> 0%
where the time goes in v3:
time: 96 us; the launch traced here: 95.7 us
  Pallas kernels  90.1 us (94%)
  local copies, waits for them, and re-layouts  4.97 us (5%)
    pallas_call x1, Pallas kernels, local(): pl.pallas_call(functools.partial(kernel, n_chan, n_tm), out_shape=jax.Sha...  90.1 us
    unnamed x2, local copies, waits for them, and re-layouts  4.2 us

profile of v3, /device:TPU:1, one launch (start us, length us, event | category | flops | bytes accessed | tf_op | source)
XLA Modules:
  0.0 95.7 jit_solution(7691806954776269812)
XLA Ops:
  0.0 0.8 reshape.6
  0.8 0.7 pad_add_fusion.pos_ref
  1.5 2.8 %copy.5 = bf16[8,8,4,2048]{3,1,2,0:T(8,128)(2,1)} copy(bf16[8,8,4,2048]{3,2,1,0:T(4,128)(2,1)} %bitcast.3) | data formatting | bytes 2097152
  4.3 90.1 %offset_stack.1 = f32[4,2048]{1,0:T(4,128)} custom-call(s32[32]{0:T(128)} %order_ref.1, s32[32,128]{1,0:T(8,128)} %pad_add_fusion.pos_ref, bf16[64,8192]{1,0:T(8,128)(2,1)} %bitcast.2, bf16[2048,2048]{1,0:T(8,128)(2,1)} %constant.2.clone.table_ref), custom_call_target="tpu_custom_call" | custom-call | tf_op jit(solution)/shard_map/offset_stack/pallas_call | solution.py:450
  94.3 1.4 %copy.7 = f32[4,2048]{1,0:T(4,128)} copy(f32[4,2048]{1,0:T(4,128)} %offset_stack.1) | data formatting | bytes 65536

commit v4 on v3

v4 whole, which is shorter than its diff:
```python
import functools

import jax
import jax.numpy as jnp
import numpy as np
from jax import lax
from jax.experimental import pallas as pl
from jax.experimental.pallas import tpu as pltpu
from jax.sharding import PartitionSpec as P

SRC = 64
STEPS = 2
SLOTS = 12
BIN_DEV = 4
MIB = 1024 * 1024

water_level = 0.1
pair_eps = 1e-06
f32 = jnp.float32
bf16 = jnp.bfloat16


def to_bins(gap, loop, bins):
    offset = jnp.minimum(gap, loop - gap)
    return jnp.floor((offset * (2 * bins) + 0.5) * (1.0 / (loop + 1)))


def block_column(pos_ref, block):
    row = pos_ref[pl.ds(block // 2, 1), :].astype(f32)
    shape = (SRC, 2 * SRC)
    from_lane = lax.broadcasted_iota(jnp.int32, shape, 1) - lax.broadcasted_iota(jnp.int32, shape, 0)
    return jnp.sum(jnp.where(from_lane == lax.rem(block, 2) * SRC, row, 0.0), axis=1, keepdims=True)


def features(x, out, double):
    re, im = x[0::2], x[1::2]
    n = 0
    for a in range(4):
        out(n, re[a] * re[a] + im[a] * im[a])
        n += 1
    for a in range(4):
        for b in range(a + 1, 4):
            real = re[a] * re[b] + im[a] * im[b]
            imag = re[a] * im[b] - im[a] * re[b]
            if double:
                real, imag = real + real, imag + imag
            out(n, real)
            out(n + 1, imag)
            n += 2


def kernel(n_chan, n_tm, order_ref, pos_ref, x_ref, table_ref, out_ref,
           sib, part, got, inv, relay, relayed, keep, crossed, ppart, pgot, pieces,
           w2, s32, fs, fr, slots, amat, hmask, wf0, wf1, t0, t1, acc,
           place, table, mine, out0, got0, out1, got1, out2, got2, got3, xk, lag_out, lag_got,
           table_sem, share_send, share_recv, send1, recv1, send2, recv2, ring_send, ring_recv, cross_send, cross_recv,
           send3, recv3, around_send, around_recv, pass_send, pass_recv,
           swap_send, swap_recv, send4, recv4, send5, recv5, send6, recv6, lag_send, lag_recv):
    rows, width = x_ref.shape
    freq = width // 8
    cols = freq // n_tm
    half = rows // 2
    bins = BIN_DEV * n_chan
    channels = n_chan * rows
    loop = float(channels + 1 + (channels - 1) // 2)
    me_c, me = lax.axis_index("chan"), lax.axis_index("tm")
    n_z = n_chan // 4
    zh, core = me_c // 2, lax.rem(me_c, 2)
    z, hi = zh // 2, lax.rem(zh, 2)
    sibling, partner = zh * 2 + 1 - core, z * 4 + (1 - hi) * 2 + core

    def above(d):
        return lax.rem(z + d + n_z, n_z)

    ways = [above(1) * 4 + hi * 2 + core, above(-1) * 4 + hi * 2 + core]
    far = n_z // 2
    reach = [[far - (w != k) for k in range(STEPS)] for w in range(2)]
    tms = [lax.rem(me + d, n_tm) for d in range(n_tm)]
    back = [lax.rem(me - d + n_tm, n_tm) for d in range(n_tm)]
    group = [(me_c, hi, tms[d]) for d in range(1, n_tm)] + [(partner, 1 - hi, tms[d]) for d in range(n_tm)]
    group_back = [(hi, back[d]) for d in range(1, n_tm)] + [(1 - hi, back[d]) for d in range(n_tm)]

    barrier = pltpu.get_barrier_semaphore()
    for chan, _, tm in group:
        pl.semaphore_signal(barrier, inc=1, device_id={"chan": chan, "tm": tm})
    pl.semaphore_signal(barrier, inc=1, device_id={"chan": sibling, "tm": me})
    for d in range(1, n_z):
        pl.semaphore_signal(barrier, inc=1, device_id={"chan": above(d) * 4 + hi * 2 + core, "tm": me})
    load = pltpu.make_async_copy(table_ref.at[pl.ds(pl.multiple_of(core * freq, freq), freq)], table, table_sem.at[0])
    load.start()
    pl.semaphore_wait(barrier, len(group) + n_z)

    def remote(src, dst, send, recv, chan, tm):
        return pltpu.make_async_remote_copy(src_ref=src, dst_ref=dst, send_sem=send, recv_sem=recv,
                                            device_id={"chan": chan, "tm": tm})

    def share(s):
        at = pl.ds(s * 4 * freq, 4 * freq)
        return remote(x_ref.at[pl.ds(pl.multiple_of((1 - core) * half, half), half), at], sib.at[:, at],
                      share_send.at[s], share_recv.at[s], sibling, me)

    for s in range(2):
        share(s).start()
    blocks = [order_ref[k] for k in range(STEPS)]
    ahead = [lax.rem(z - blocks[k] // 4 + n_z, n_z) for k in range(STEPS)]
    own_core = [lax.rem(blocks[k], 2) == core for k in range(STEPS)]
    mine_at = pl.ds(pl.multiple_of(core * half, half), half)
    subs = [(k, s) for s in range(2) for k in range(STEPS)]

    def own(k, n, plane):
        at = pl.ds(pl.multiple_of(n * freq + plane * 128, 128), 128)
        return jnp.where(own_core[k], x_ref[mine_at, at], sib[:, at])

    def hop(w, t, k, s):
        n = pl.ds(s * 4, 4)
        return remote(relay.at[w, t, k, n], relayed.at[w, t, k, n], ring_send.at[w, t, 2 * k + s],
                      ring_recv.at[w, t, 2 * k + s], ways[w], me)

    def ring_round(t, between=()):
        for k, s in subs:
            if t == 0 and k == 0:
                share(s).wait()
            for w in range(2):
                if t >= reach[w][k]:
                    continue
                plane = above(reach[w][k] - t) if w == 0 else above(t - reach[w][k])
                if t:
                    hop(w, t - 1, k, s).wait_recv()
                for n in range(s * 4, s * 4 + 4):
                    value = own(k, n, plane)
                    if t:
                        value = jnp.where(ahead[k] == 0, value, relayed[w, t - 1, k, n])
                    relay[w, t, k, n] = value
                hop(w, t, k, s).start()
            if between:
                between.pop(0)()

    def power(first_p, last_p):
        for p in range(first_p, last_p):
            total = None
            for n in range(8):
                v = x_ref[:, n * freq + p * cols:n * freq + (p + 1) * cols].astype(f32)
                total = v * v if total is None else total + v * v
            part[p] = total

    first = [remote(part.at[tms[d]], got.at[me], send1.at[d], recv1.at[me], me_c, tms[d]) for d in range(1, n_tm)]

    def send_power():
        power(n_tm // 2, n_tm)
        for copy in first:
            copy.start()

    counts = []

    def count_pairs(k):
        src = block_column(pos_ref, blocks[k])

        def count(i, sums):
            pair_bins = to_bins(jnp.abs(src - pos_ref[pl.ds(i, 1), :].astype(f32)), loop, bins)
            rel = pair_bins - (me_c * BIN_DEV).astype(f32)
            return tuple(s + jnp.where(rel == float(b), 1.0, 0.0) for b, s in enumerate(sums))

        init = tuple(jnp.zeros((SRC, pos_ref.shape[1]), f32) for _ in range(BIN_DEV))
        counts.append(lax.fori_loop(0, pos_ref.shape[0], count, init))

    ring_round(0, [functools.partial(power, 0, n_tm // 2), send_power,
                   functools.partial(count_pairs, 0), functools.partial(count_pairs, 1)])
    factors = []
    for b in range(BIN_DEV):
        amount = sum(c[b] for c in counts)
        amount = jnp.sum(jnp.sum(amount, axis=1, keepdims=True), axis=0, keepdims=True)
        alone = jnp.where(me_c * BIN_DEV + b == 0, float(STEPS * SRC), 0.0)
        factors.append(lax.rsqrt((amount - alone) * float(n_tm * freq)))
    norm = jnp.concatenate(factors, 0)

    ring_round(1)

    lane = lax.broadcasted_iota(jnp.int32, (SRC, 2 * rows), 1)
    rec = pos_ref[pl.ds(zh, 1), :].astype(f32)
    rec = jnp.where(lane[:1] // rows == core, rec, pltpu.roll(rec, rows, axis=1))
    rec_ids = me_c * rows + lane % rows
    span = 2 * SLOTS
    col = lax.broadcasted_iota(jnp.int32, (bins, 2 * STEPS * span), 1)
    row = lax.broadcasted_iota(jnp.int32, (bins, 2 * STEPS * span), 0).astype(f32)
    inner = col % span
    marked = inner >= SLOTS
    first_bin = jnp.zeros((1, 1), f32)
    for step in range(STEPS):
        block = blocks[step]
        pair_bins = to_bins(jnp.abs(block_column(pos_ref, block) - rec), loop, bins)
        src_ids = block * SRC + lax.broadcasted_iota(jnp.int32, (SRC, 2 * rows), 0)
        lowest = jnp.min(jnp.min(pair_bins, axis=1, keepdims=True), axis=0, keepdims=True)
        first_bin = jnp.where(col < step * 2 * span, first_bin, lowest)
        rel = pair_bins - lowest
        upper = rel >= float(SLOTS)
        slot = jnp.where(upper, rel - float(SLOTS), rel)
        slots[step] = jnp.where(src_ids == rec_ids, -1.0, slot)
        for k in range(SLOTS):
            mark = jnp.max(jnp.where((slot == float(k)) & upper, 1.0, 0.0), axis=1, keepdims=True)
            hmask[step, k * SRC:(k + 1) * SRC, :] = jnp.broadcast_to(mark, (SRC, 128))
    at = first_bin + (inner - jnp.where(marked, SLOTS, 0)).astype(f32)
    lower = jnp.where(row == at, 1.0, 0.0)
    place[...] = jnp.where(marked, jnp.where(row == at + float(SLOTS), 1.0, 0.0) - lower, lower).astype(bf16)

    ring_round(2)

    total = part[me]
    for d in range(1, n_tm):
        remote(part.at[me], got.at[back[d]], send1.at[d], recv1.at[back[d]], me_c, tms[d]).wait_recv()
        total = total + got[back[d]]
    inv[me] = 1.0 / jnp.sqrt(total * (1.0 / (4 * n_tm)) + water_level)
    second = [remote(inv.at[me], inv.at[me], send2.at[d], recv2.at[me], me_c, tms[d]) for d in range(1, n_tm)]
    for copy in second:
        copy.start()

    for t in range(3, far):
        ring_round(t)

    cross = [remote(keep.at[k], crossed.at[k], cross_send.at[k], cross_recv.at[k], partner, me) for k in range(STEPS)]
    for k in range(STEPS):
        total = None
        for s in range(2):
            for w in range(2):
                hop(w, reach[w][k] - 1, k, s).wait_recv()
            for n in range(s * 4, s * 4 + 4):
                value = jnp.where(ahead[k] <= reach[0][k], relayed[0, reach[0][k] - 1, k, n],
                                  relayed[1, reach[1][k] - 1, k, n])
                value = jnp.where(ahead[k] == 0, own(k, n, z), value)
                keep[k, n] = value
                value = value.astype(f32)
                total = value * value if total is None else total + value * value
        cross[k].start()
        ppart[k * half:(k + 1) * half] = total.astype(bf16)
    spot = hi * n_tm + me
    third = [remote(ppart, pgot.at[spot], send3.at[i], recv3.at[spot], chan, tm)
             for i, (chan, _, tm) in enumerate(group)]
    for copy in third[::-1]:
        copy.start()

    def whiten(p):
        factor = inv[p]
        for n in range(8):
            at = pl.ds(pl.multiple_of(n * freq + p * cols, cols), cols)
            value = (x_ref[:, at].astype(f32) * factor).astype(bf16)
            w2[:rows, at] = value
            w2[rows:, at] = value

    whiten(me)
    for d in range(1, n_tm):
        remote(inv.at[me], inv.at[back[d]], send2.at[d], recv2.at[back[d]], me_c, tms[d]).wait_recv()
        whiten(back[d])

    def receiver_features(i, _):
        for r in range(0, rows, 16):
            x = [w2[r:r + 16, pl.ds(pl.multiple_of(n * freq + i * 128, 128), 128)].astype(f32) for n in range(8)]

            def out(n, value):
                value = value.astype(bf16)
                fr[i, r:r + 16, n * 128:(n + 1) * 128] = value
                fr[i, rows + r:rows + r + 16, n * 128:(n + 1) * 128] = value

            features(x, out, True)
        return 0

    sums = [ppart[...].astype(f32), jnp.zeros(ppart.shape, f32)]
    for i, ((chan, _, tm), (h, t)) in enumerate(zip(group, group_back)):
        other = h * n_tm + t
        remote(ppart, pgot.at[other], send3.at[i], recv3.at[other], chan, tm).wait_recv()
        side = 0 if i < n_tm - 1 else 1
        sums[side] = sums[side] + pgot[other].astype(f32)
    for k in range(STEPS):
        from_here = lax.rem(blocks[k] // 2, 2) == hi
        at = slice(k * half, (k + 1) * half)
        total = jnp.where(from_here, sums[0][at], sums[1][at])
        factor = 1.0 / jnp.sqrt(total * (1.0 / (4 * n_tm)) + water_level)
        cross[k].wait()
        for n in range(8):
            value = jnp.where(from_here, keep[k, n], crossed[k, n])
            pieces[core, z, k, n] = (value.astype(f32) * factor).astype(bf16)

    def around(w, t, k, s, arriving):
        d = t + 1 if arriving else t
        ref = pieces.at[core, above(-d) if w == 0 else above(d), k, pl.ds(s * 4, 4)]
        return remote(ref, ref, around_send.at[w, t, 2 * k + s], around_recv.at[w, t, 2 * k + s], ways[w], me)

    def pass_over(d, c):
        ref = pieces.at[c, above(d)]
        slot = d + n_z // 2
        return remote(ref, ref, pass_send.at[slot], pass_recv.at[slot], sibling, me)

    def add_energy(d, energy):
        pass_over(d, 1 - core).wait_recv()
        plane = above(d)
        for k in range(STEPS):
            for q in range(4):
                r = k * SRC + q * 16
                x = [pieces[q // 2, plane, k, n, (q % 2) * 16:(q % 2) * 16 + 16, :].astype(f32) for n in range(8)]
                for n in range(8):
                    s32[plane, n, r:r + 16, :] = x[n]

                def out(n, value):
                    fs[r:r + 16, n * 128:(n + 1) * 128] = value.astype(bf16)

                features(x, out, False)
        return energy + lax.dot_general(fs[...], fr[plane], (((1,), (1,)), ((), ())), preferred_element_type=f32)

    for k, s in subs:
        for w in range(2):
            around(w, 0, k, s, False).start()
        if (k, s) == subs[0]:
            pass_over(0, core).start()
        at = subs.index((k, s))
        lax.fori_loop(at * n_z // 4, (at + 1) * n_z // 4, receiver_features, 0)
    energy = jnp.zeros((STEPS * SRC, 2 * rows), f32)
    for t in range(1, far + 1):
        if t == far:
            energy = add_energy(1 - t, energy)
            energy = add_energy(t - 1, energy)
        for k, s in subs:
            for w in range(2):
                if t <= reach[w][k]:
                    around(w, t - 1, k, s, True).wait_recv()
                if t < reach[w][k]:
                    around(w, t, k, s, False).start()
        pass_over(-t, core).start()
        if t < far:
            pass_over(t, core).start()
            energy = add_energy(1 - t, energy)
            if t > 1:
                energy = add_energy(t - 1, energy)
    energy = add_energy(-far, energy)
    scale = lax.rsqrt(jnp.maximum(energy, 0.0) * (1.0 / (2 * freq)) + pair_eps)

    for step in range(STEPS):
        weight = scale[step * SRC:(step + 1) * SRC]
        slot = slots[step]
        for k in range(SLOTS):
            value = jnp.where(slot == float(k), weight, 0.0)
            high = value.astype(bf16).astype(f32)
            amat[step, k * SRC:(k + 1) * SRC, :] = jnp.where(lane < rows, high, value - high).astype(bf16)

    def project(step, chunk, wf, t):
        for n in range(8):
            wf[:, n * 128:(n + 1) * 128] = w2[:, pl.ds(pl.multiple_of(n * freq + chunk * 128, 128), 128)]
        t[...] = jnp.dot(amat[step], wf[...], preferred_element_type=f32)

    def gather(step, chunk, t):
        for k in range(SLOTS):
            sums = [None] * 4
            for g in range(SRC // 8):
                r = k * SRC + g * 8
                row = step * SRC + g * 8
                re, im = [], []
                for a in range(4):
                    tr = t[r:r + 8, 2 * a * 128:(2 * a + 1) * 128]
                    ti = t[r:r + 8, (2 * a + 1) * 128:(2 * a + 2) * 128]
                    sr = s32[chunk, 2 * a, row:row + 8, :]
                    si = s32[chunk, 2 * a + 1, row:row + 8, :]
                    re += [sr * tr, si * ti]
                    im.append(sr * ti - si * tr)
                real = ((re[0] + re[1]) + (re[2] + re[3])) + ((re[4] + re[5]) + (re[6] + re[7]))
                imag = (im[0] + im[1]) + (im[2] + im[3])
                mark = hmask[step, r:r + 8, :]
                new = [real, imag, real * mark, imag * mark]
                sums = new if g == 0 else [x + y for x, y in zip(sums, new)]
            for n in range(2):
                base = n * SLOTS * 8 + k * 8
                acc[step, base:base + 8, :128] = sums[2 * n]
                acc[step, base:base + 8, 128:] = sums[2 * n + 1]

    def swap(p):
        return remote(out0.at[p], got0.at[p], swap_send.at[p], swap_recv.at[p], sibling, me)

    def to_owner(p, h):
        return remote(out1.at[p, h], got1.at[spot], send4.at[p, h], recv4.at[spot], z * 4 + h * 2 + core, p)

    def to_owners(p, act):
        for h in range(2):
            @pl.when((p != me) | (hi != h))
            def _():
                act(to_owner(p, h))

    def hand_on(p):
        swap(p).wait_recv()
        value = (mine[p] + got0[p].astype(f32)).reshape(n_z, 2, 8, cols)
        for h in range(2):
            out1[p, h] = value[:, h].reshape(bins // 2, cols).astype(bf16)
        to_owners(p, lambda copy: copy.start())

    project(0, 0, wf0, t0)

    def one_chunk(p, _):
        project(1, p, wf1, t1)
        gather(0, p, t0)
        project(0, jnp.minimum(p + 1, n_tm - 1), wf0, t0)
        gather(1, p, t1)
        rows_of = []
        for step in range(STEPS):
            value = jnp.sum(acc[step].reshape(span, 8, 256), axis=1)
            high = value.astype(bf16).astype(f32)
            rows_of += [high, value - high]
        out = jnp.dot(place[...], jnp.concatenate(rows_of, 0).astype(bf16), preferred_element_type=f32)
        mine[p] = jnp.where(core == 0, out[:, :128], out[:, 128:])
        out0[p] = jnp.where(core == 0, out[:, 128:], out[:, :128]).astype(bf16)
        swap(p).start()

        @pl.when(p > 0)
        def _():
            hand_on(p - 1)

        return 0

    lax.fori_loop(0, n_tm, one_chunk, 0)
    hand_on(n_tm - 1)
    total = out1[me, hi].astype(f32)
    for (chan, _, tm), (h, t) in zip(group, group_back):
        other = h * n_tm + t
        remote(out1.at[me, hi], got1.at[other], send4.at[me, hi], recv4.at[other], chan, tm).wait_recv()
        total = total + got1[other].astype(f32)
    out2[...] = total.reshape(out2.shape)

    def to_plane(d):
        return remote(out2.at[above(d)], got2.at[z], send5.at[d], recv5.at[z], above(d) * 4 + hi * 2 + core, me)

    for d in sorted(range(1, n_z), key=lambda d: -min(d, n_z - d)):
        to_plane(d).start()
    total = out2[z]
    for d in range(1, n_z):
        other = above(-d)
        remote(out2.at[z], got2.at[other], send5.at[d], recv5.at[other], above(d) * 4 + hi * 2 + core, me).wait_recv()
        total = total + got2[other]
    got3[me] = total
    fifth = [remote(got3.at[me], got3.at[me], send6.at[d], recv6.at[me], me_c, tms[d]) for d in range(1, n_tm)]
    for copy in fifth:
        copy.start()
    for d in range(1, n_tm):
        remote(got3.at[me], got3.at[back[d]], send6.at[d], recv6.at[back[d]], me_c, tms[d]).wait_recv()
    for n in range(n_tm):
        value = got3[n]
        high = value.astype(bf16).astype(f32)
        xk[:, n * cols:(n + 1) * cols] = jnp.concatenate([high, value - high], 0).astype(bf16)
    load.wait()
    lag = 512

    def lag_swap(i):
        return remote(lag_out.at[i], lag_got.at[i], lag_send.at[i], lag_recv.at[i], sibling, me)

    for i in range(2 * freq // lag):
        both = jnp.dot(xk[...], table[:, i * lag:(i + 1) * lag], preferred_element_type=f32)
        both = both[:8] + both[8:]
        lag_out[i] = jnp.where(core == 0, both[BIN_DEV:], both[:BIN_DEV])
        lag_swap(i).start()
        out_ref[:, i * lag:(i + 1) * lag] = jnp.where(core == 0, both[:BIN_DEV], both[BIN_DEV:])
    for i in range(2 * freq // lag):
        lag_swap(i).wait_recv()
        at = slice(i * lag, (i + 1) * lag)
        out_ref[:, at] = (out_ref[:, at] + lag_got[i]) * norm

    for w in range(2):
        for k, s in subs:
            for t in range(reach[w][k]):
                hop(w, t, k, s).wait_send()
                around(w, t, k, s, False).wait_send()
    for d in range(-far, far):
        pass_over(d, core).wait_send()
    for p in range(n_tm):
        swap(p).wait_send()
        to_owners(p, lambda copy: copy.wait_send())

    for d in range(1, n_z):
        to_plane(d).wait_send()
    for i in range(2 * freq // lag):
        lag_swap(i).wait_send()
    for copy in first + second + third + fifth:
        copy.wait_send()


def lag_table(freq):
    width = 2 * freq
    phase = np.outer(np.arange(freq), np.arange(width) - freq) % width
    angle = 2.0 * np.pi / width * phase
    return np.concatenate([np.cos(angle), -np.sin(angle)], 0).astype(jnp.bfloat16)


def local(spectra, positions, source_order):
    rows, seg_dev, lags = spectra.shape
    n_chan = lax.axis_size("chan")
    n_tm = lax.axis_size("tm")
    bins = BIN_DEV * n_chan
    flat = spectra.reshape(rows, seg_dev * lags)
    pos2 = positions.reshape(n_chan // 2, 2 * rows)
    width = seg_dev * lags
    freq = lags // 2
    cols = freq // n_tm
    n_z = n_chan // 4
    half = rows // 2
    up = n_z // 2
    vm = pl.BlockSpec(memory_space=pltpu.VMEM)
    dma = pltpu.SemaphoreType.DMA
    vmem = pltpu.VMEM
    return pl.pallas_call(
        functools.partial(kernel, n_chan, n_tm),
        out_shape=jax.ShapeDtypeStruct((BIN_DEV, lags), f32),
        in_specs=[pl.BlockSpec(memory_space=pltpu.SMEM), vm, vm, pl.BlockSpec(memory_space=pl.ANY)],
        out_specs=vm,
        scratch_shapes=[
            vmem((half, width), bf16),
            vmem((n_tm, rows, cols), f32),
            vmem((n_tm, rows, cols), f32),
            vmem((n_tm, rows, cols), f32),
            vmem((2, up, STEPS, 8, half, 128), bf16),
            vmem((2, up, STEPS, 8, half, 128), bf16),
            vmem((STEPS, 8, half, 128), bf16),
            vmem((STEPS, 8, half, 128), bf16),
            vmem((STEPS * half, 128), bf16),
            vmem((2 * n_tm, STEPS * half, 128), bf16),
            vmem((2, n_z, STEPS, 8, half, 128), bf16),
            vmem((2 * rows, width), bf16),
            vmem((n_z, 8, STEPS * SRC, 128), f32),
            vmem((STEPS * SRC, 16 * 128), bf16),
            vmem((n_z, 2 * rows, 16 * 128), bf16),
            vmem((STEPS, SRC, 2 * rows), f32),
            vmem((STEPS, SLOTS * SRC, 2 * rows), bf16),
            vmem((STEPS, SLOTS * SRC, 128), f32),
            vmem((2 * rows, 1024), bf16),
            vmem((2 * rows, 1024), bf16),
            vmem((SLOTS * SRC, 1024), f32),
            vmem((SLOTS * SRC, 1024), f32),
            vmem((STEPS, 2 * SLOTS * 8, 256), f32),
            vmem((bins, 4 * STEPS * SLOTS), bf16),
            vmem((freq, lags), bf16),
            vmem((n_tm, bins, cols), f32),
            vmem((n_tm, bins, cols), bf16),
            vmem((n_tm, bins, cols), bf16),
            vmem((n_tm, 2, bins // 2, cols), bf16),
            vmem((2 * n_tm, bins // 2, cols), bf16),
            vmem((n_z, bins // n_z // 2, cols), f32),
            vmem((n_z, bins // n_z // 2, cols), f32),
            vmem((n_tm, bins // n_z // 2, cols), f32),
            vmem((16, freq), bf16),
            vmem((4, BIN_DEV, lags // 4), f32),
            vmem((4, BIN_DEV, lags // 4), f32),
            dma((1,)), dma((2,)), dma((2,)), dma((n_tm,)), dma((n_tm,)), dma((n_tm,)), dma((n_tm,)),
            dma((2, up, 4)), dma((2, up, 4)), dma((2,)), dma((2,)), dma((2 * n_tm,)), dma((2 * n_tm,)),
            dma((2, up, 4)), dma((2, up, 4)), dma((n_z,)), dma((n_z,)),
            dma((n_tm,)), dma((n_tm,)), dma((n_tm, 2)), dma((2 * n_tm,)), dma((n_z,)), dma((n_z,)),
            dma((n_tm,)), dma((n_tm,)), dma((4,)), dma((4,)),
        ],
        compiler_params=pltpu.CompilerParams(collective_id=0, has_side_effects=True, vmem_limit_bytes=58 * MIB),
        name="offset_stack",
    )(source_order, pos2, flat, jnp.asarray(lag_table(freq)))


def solution(mesh):
    return jax.shard_map(
        local,
        mesh=mesh,
        in_specs=(P("chan", "tm", None), P(), P()),
        out_specs=P("chan", None),
        check_vma=False,
    )
```

time: 96 us -> 90.9 us (0.947)
  Pallas kernels: 90.1 us -> 86.4 us
    pallas_call x1, Pallas kernels: 90.1 us -> 86.4 us  [local(): pl.pallas_call(functools.partial(kernel, n_chan, n_tm), out_shape=jax.Sha...]
where the time goes in v4:
time: 90.9 us; the launch traced here: 90.7 us
  Pallas kernels  86.4 us (95%)
  local copies, waits for them, and re-layouts  4.2 us (5%)
    pallas_call x1, Pallas kernels, local(): pl.pallas_call(functools.partial(kernel, n_chan, n_tm), out_shape=jax.Sha...  86.4 us
    unnamed x2, local copies, waits for them, and re-layouts  4.2 us

profile of v4, /device:TPU:1, one launch (start us, length us, event | category | flops | bytes accessed | tf_op | source)
XLA Modules:
  0.0 90.7 jit_solution(10131946934516908569)
XLA Ops:
  0.0 2.8 %copy.5 = bf16[8,8,4,2048]{3,1,2,0:T(8,128)(2,1)} copy(bf16[8,8,4,2048]{3,2,1,0:T(4,128)(2,1)} %bitcast.4) | data formatting | bytes 2097152
  2.8 86.4 %offset_stack.1 = f32[4,2048]{1,0:T(4,128)} custom-call(s32[32]{0:T(128)} %order_ref.1, s32[16,128]{1,0:T(8,128)} %bitcast.5, bf16[64,8192]{1,0:T(8,128)(2,1)} %bitcast.3, bf16[2048,2048]{1,0:T(8,128)(2,1)} %constant.2.clone.table_ref), custom_call_target="tpu_custom_call" | custom-call | tf_op jit(solution)/shard_map/offset_stack/pallas_call | solution.py:501
  89.3 1.4 %copy.7 = f32[4,2048]{1,0:T(4,128)} copy(f32[4,2048]{1,0:T(4,128)} %offset_stack.1) | data formatting | bytes 65536

commit v5 on v4

--- a/solution.py
+++ b/solution.py
@@ -12,6 +12,7 @@
 STEPS = 2
 SLOTS = 12
 BIN_DEV = 4
+PARTS = 2
 MIB = 1024 * 1024
 
 water_level = 0.1
@@ -49,11 +50,11 @@
             n += 2
 
 
-def kernel(n_chan, n_tm, order_ref, pos_ref, x_ref, table_ref, out_ref,
-           sib, part, got, inv, relay, relayed, keep, crossed, ppart, pgot, pieces,
+def kernel(n_chan, n_tm, order_ref, pos_ref, spectra_ref, table_ref, out_ref,
+           raw, x_ref, sib, part, got, inv, relay, relayed, keep, crossed, ppart, pgot, pieces,
            w2, s32, fs, fr, slots, amat, hmask, wf0, wf1, t0, t1, acc,
            place, table, mine, out0, got0, out1, got1, out2, got2, got3, xk, lag_out, lag_got,
-           table_sem, share_send, share_recv, send1, recv1, send2, recv2, ring_send, ring_recv, cross_send, cross_recv,
+           table_sem, raw_sem, share_send, share_recv, send1, recv1, send2, recv2, ring_send, ring_recv, cross_send, cross_recv,
            send3, recv3, around_send, around_recv, pass_send, pass_recv,
            swap_send, swap_recv, send4, recv4, send5, recv5, send6, recv6, lag_send, lag_recv):
     rows, width = x_ref.shape
@@ -87,7 +88,13 @@
     for d in range(1, n_z):
         pl.semaphore_signal(barrier, inc=1, device_id={"chan": above(d) * 4 + hi * 2 + core, "tm": me})
     load = pltpu.make_async_copy(table_ref.at[pl.ds(pl.multiple_of(core * freq, freq), freq)], table, table_sem.at[0])
+    fetch = pltpu.make_async_copy(spectra_ref, raw, raw_sem.at[0])
+    fetch.start()
+    fetch.wait()
     load.start()
+    lags = raw.shape[2]
+    for a in range(raw.shape[1]):
+        x_ref[:, a * lags:(a + 1) * lags] = raw[:, a, :]
     pl.semaphore_wait(barrier, len(group) + n_z)
 
     def remote(src, dst, send, recv, chan, tm):
@@ -105,28 +112,29 @@
     ahead = [lax.rem(z - blocks[k] // 4 + n_z, n_z) for k in range(STEPS)]
     own_core = [lax.rem(blocks[k], 2) == core for k in range(STEPS)]
     mine_at = pl.ds(pl.multiple_of(core * half, half), half)
-    subs = [(k, s) for s in range(2) for k in range(STEPS)]
+    subs = [(k, s) for s in range(PARTS) for k in range(STEPS)]
+    per = 8 // PARTS
 
     def own(k, n, plane):
         at = pl.ds(pl.multiple_of(n * freq + plane * 128, 128), 128)
         return jnp.where(own_core[k], x_ref[mine_at, at], sib[:, at])
 
     def hop(w, t, k, s):
-        n = pl.ds(s * 4, 4)
-        return remote(relay.at[w, t, k, n], relayed.at[w, t, k, n], ring_send.at[w, t, 2 * k + s],
-                      ring_recv.at[w, t, 2 * k + s], ways[w], me)
+        n = pl.ds(s * per, per)
+        return remote(relay.at[w, t, k, n], relayed.at[w, t, k, n], ring_send.at[w, t, k * PARTS + s],
+                      ring_recv.at[w, t, k * PARTS + s], ways[w], me)
 
     def ring_round(t, between=()):
         for k, s in subs:
-            if t == 0 and k == 0:
-                share(s).wait()
+            if t == 0 and k == 0 and s % (PARTS // 2) == 0:
+                share(s // (PARTS // 2)).wait()
             for w in range(2):
                 if t >= reach[w][k]:
                     continue
                 plane = above(reach[w][k] - t) if w == 0 else above(t - reach[w][k])
                 if t:
                     hop(w, t - 1, k, s).wait_recv()
-                for n in range(s * 4, s * 4 + 4):
+                for n in range(s * per, (s + 1) * per):
                     value = own(k, n, plane)
                     if t:
                         value = jnp.where(ahead[k] == 0, value, relayed[w, t - 1, k, n])
@@ -145,11 +153,6 @@
 
     first = [remote(part.at[tms[d]], got.at[me], send1.at[d], recv1.at[me], me_c, tms[d]) for d in range(1, n_tm)]
 
-    def send_power():
-        power(n_tm // 2, n_tm)
-        for copy in first:
-            copy.start()
-
     counts = []
 
     def count_pairs(k):
@@ -163,8 +166,12 @@
         init = tuple(jnp.zeros((SRC, pos_ref.shape[1]), f32) for _ in range(BIN_DEV))
         counts.append(lax.fori_loop(0, pos_ref.shape[0], count, init))
 
-    ring_round(0, [functools.partial(power, 0, n_tm // 2), send_power,
-                   functools.partial(count_pairs, 0), functools.partial(count_pairs, 1)])
+    step = n_tm // len(subs)
+    ring_round(0, [functools.partial(power, i * step, (i + 1) * step) for i in range(len(subs))])
+    for copy in first:
+        copy.start()
+    for k in range(STEPS):
+        count_pairs(k)
     factors = []
     for b in range(BIN_DEV):
         amount = sum(c[b] for c in counts)
@@ -219,10 +226,10 @@
     cross = [remote(keep.at[k], crossed.at[k], cross_send.at[k], cross_recv.at[k], partner, me) for k in range(STEPS)]
     for k in range(STEPS):
         total = None
-        for s in range(2):
+        for s in range(PARTS):
             for w in range(2):
                 hop(w, reach[w][k] - 1, k, s).wait_recv()
-            for n in range(s * 4, s * 4 + 4):
+            for n in range(s * per, (s + 1) * per):
                 value = jnp.where(ahead[k] <= reach[0][k], relayed[0, reach[0][k] - 1, k, n],
                                   relayed[1, reach[1][k] - 1, k, n])
                 value = jnp.where(ahead[k] == 0, own(k, n, z), value)
@@ -280,8 +287,8 @@
 
     def around(w, t, k, s, arriving):
         d = t + 1 if arriving else t
-        ref = pieces.at[core, above(-d) if w == 0 else above(d), k, pl.ds(s * 4, 4)]
-        return remote(ref, ref, around_send.at[w, t, 2 * k + s], around_recv.at[w, t, 2 * k + s], ways[w], me)
+        ref = pieces.at[core, above(-d) if w == 0 else above(d), k, pl.ds(s * per, per)]
+        return remote(ref, ref, around_send.at[w, t, k * PARTS + s], around_recv.at[w, t, k * PARTS + s], ways[w], me)
 
     def pass_over(d, c):
         ref = pieces.at[c, above(d)]
@@ -310,7 +317,7 @@
         if (k, s) == subs[0]:
             pass_over(0, core).start()
         at = subs.index((k, s))
-        lax.fori_loop(at * n_z // 4, (at + 1) * n_z // 4, receiver_features, 0)
+        lax.fori_loop(at * n_z // len(subs), (at + 1) * n_z // len(subs), receiver_features, 0)
     energy = jnp.zeros((STEPS * SRC, 2 * rows), f32)
     for t in range(1, far + 1):
         if t == far:
@@ -331,7 +338,7 @@
     energy = add_energy(-far, energy)
     scale = lax.rsqrt(jnp.maximum(energy, 0.0) * (1.0 / (2 * freq)) + pair_eps)
 
-    for step in range(STEPS):
+    def weigh(step):
         weight = scale[step * SRC:(step + 1) * SRC]
         slot = slots[step]
         for k in range(SLOTS):
@@ -387,12 +394,18 @@
             out1[p, h] = value[:, h].reshape(bins // 2, cols).astype(bf16)
         to_owners(p, lambda copy: copy.start())
 
-    project(0, 0, wf0, t0)
-
-    def one_chunk(p, _):
+    def chunk(q):
+        return lax.rem(me + 1 + q, n_tm)
+
+    weigh(0)
+    project(0, chunk(0), wf0, t0)
+    weigh(1)
+
+    def one_chunk(q, _):
+        p = chunk(q)
         project(1, p, wf1, t1)
         gather(0, p, t0)
-        project(0, jnp.minimum(p + 1, n_tm - 1), wf0, t0)
+        project(0, chunk(q + 1), wf0, t0)
         gather(1, p, t1)
         rows_of = []
         for step in range(STEPS):
@@ -404,14 +417,14 @@
         out0[p] = jnp.where(core == 0, out[:, 128:], out[:, :128]).astype(bf16)
         swap(p).start()
 
-        @pl.when(p > 0)
+        @pl.when(q > 0)
         def _():
-            hand_on(p - 1)
+            hand_on(chunk(q - 1))
 
         return 0
 
     lax.fori_loop(0, n_tm, one_chunk, 0)
-    hand_on(n_tm - 1)
+    hand_on(me)
     total = out1[me, hi].astype(f32)
     for (chan, _, tm), (h, t) in zip(group, group_back):
         other = h * n_tm + t
@@ -487,7 +500,6 @@
     n_chan = lax.axis_size("chan")
     n_tm = lax.axis_size("tm")
     bins = BIN_DEV * n_chan
-    flat = spectra.reshape(rows, seg_dev * lags)
     pos2 = positions.reshape(n_chan // 2, 2 * rows)
     width = seg_dev * lags
     freq = lags // 2
@@ -496,14 +508,17 @@
     half = rows // 2
     up = n_z // 2
     vm = pl.BlockSpec(memory_space=pltpu.VMEM)
+    hbm = pl.BlockSpec(memory_space=pl.ANY)
     dma = pltpu.SemaphoreType.DMA
     vmem = pltpu.VMEM
     return pl.pallas_call(
         functools.partial(kernel, n_chan, n_tm),
         out_shape=jax.ShapeDtypeStruct((BIN_DEV, lags), f32),
-        in_specs=[pl.BlockSpec(memory_space=pltpu.SMEM), vm, vm, pl.BlockSpec(memory_space=pl.ANY)],
+        in_specs=[pl.BlockSpec(memory_space=pltpu.SMEM), vm, hbm, hbm],
         out_specs=vm,
         scratch_shapes=[
+            vmem((rows, seg_dev, lags), bf16),
+            vmem((rows, width), bf16),
             vmem((half, width), bf16),
             vmem((n_tm, rows, cols), f32),
             vmem((n_tm, rows, cols), f32),
@@ -540,15 +555,15 @@
             vmem((16, freq), bf16),
             vmem((4, BIN_DEV, lags // 4), f32),
             vmem((4, BIN_DEV, lags // 4), f32),
-            dma((1,)), dma((2,)), dma((2,)), dma((n_tm,)), dma((n_tm,)), dma((n_tm,)), dma((n_tm,)),
-            dma((2, up, 4)), dma((2, up, 4)), dma((2,)), dma((2,)), dma((2 * n_tm,)), dma((2 * n_tm,)),
-            dma((2, up, 4)), dma((2, up, 4)), dma((n_z,)), dma((n_z,)),
+            dma((1,)), dma((1,)), dma((2,)), dma((2,)), dma((n_tm,)), dma((n_tm,)), dma((n_tm,)), dma((n_tm,)),
+            dma((2, up, STEPS * PARTS)), dma((2, up, STEPS * PARTS)), dma((2,)), dma((2,)), dma((2 * n_tm,)), dma((2 * n_tm,)),
+            dma((2, up, STEPS * PARTS)), dma((2, up, STEPS * PARTS)), dma((n_z,)), dma((n_z,)),
             dma((n_tm,)), dma((n_tm,)), dma((n_tm, 2)), dma((2 * n_tm,)), dma((n_z,)), dma((n_z,)),
             dma((n_tm,)), dma((n_tm,)), dma((4,)), dma((4,)),
         ],
         compiler_params=pltpu.CompilerParams(collective_id=0, has_side_effects=True, vmem_limit_bytes=58 * MIB),
         name="offset_stack",
-    )(source_order, pos2, flat, jnp.asarray(lag_table(freq)))
+    )(source_order, pos2, spectra, jnp.asarray(lag_table(freq)))
 
 
 def solution(mesh):

time: 90.9 us -> 86.4 us (0.950)
  local copies, waits for them, and re-layouts: 4.2 us -> 1.38 us
  Pallas kernels: 86.4 us -> 84.8 us
    unnamed x2 -> x1, local copies, waits for them, and re-layouts: 4.2 us -> 1.38 us
    pallas_call x1, Pallas kernels: 86.4 us -> 84.8 us  [local(): pl.pallas_call(functools.partial(kernel, n_chan, n_tm), out_shape=jax.Sha...]
where the time goes in v5:
time: 86.4 us; the launch traced here: 86.2 us
  Pallas kernels  84.8 us (98%)
  local copies, waits for them, and re-layouts  1.38 us (2%)
    pallas_call x1, Pallas kernels, local(): pl.pallas_call(functools.partial(kernel, n_chan, n_tm), out_shape=jax.Sha...  84.8 us

profile of v5, /device:TPU:1, one launch (start us, length us, event | category | flops | bytes accessed | tf_op | source)
XLA Modules:
  0.0 86.2 jit_solution(5067392356332648348)
XLA Ops:
  0.0 84.8 %offset_stack.1 = f32[4,2048]{1,0:T(4,128)} custom-call(s32[32]{0:T(128)} %order_ref.1, s32[16,128]{1,0:T(8,128)} %bitcast.1, bf16[64,4,2048]{2,1,0:T(4,128)(2,1)} %spectra_ref.1, bf16[2048,2048]{1,0:T(8,128)(2,1)} %constant.2.clone.table_ref), custom_call_target="tpu_custom_call" | custom-call | tf_op jit(solution)/shard_map/offset_stack/pallas_call | solution.py:514
  84.8 1.4 %copy.6 = f32[4,2048]{1,0:T(4,128)} copy(f32[4,2048]{1,0:T(4,128)} %offset_stack.1) | data formatting | bytes 65536

commit v6 on v5

--- a/solution.py
+++ b/solution.py
@@ -53,10 +53,10 @@
 def kernel(n_chan, n_tm, order_ref, pos_ref, spectra_ref, table_ref, out_ref,
            raw, x_ref, sib, part, got, inv, relay, relayed, keep, crossed, ppart, pgot, pieces,
            w2, s32, fs, fr, slots, amat, hmask, wf0, wf1, t0, t1, acc,
-           place, table, mine, out0, got0, out1, got1, out2, got2, got3, xk, lag_out, lag_got,
+           place, table, mine, out0, got0, out1, got1, last_out, last_got, out2, got2, got3, xk, lag_out, lag_got,
            table_sem, raw_sem, share_send, share_recv, send1, recv1, send2, recv2, ring_send, ring_recv, cross_send, cross_recv,
            send3, recv3, around_send, around_recv, pass_send, pass_recv,
-           swap_send, swap_recv, send4, recv4, send5, recv5, send6, recv6, lag_send, lag_recv):
+           swap_send, swap_recv, send4, recv4, send5, recv5, last_send, last_recv, send6, recv6, lag_send, lag_recv):
     rows, width = x_ref.shape
     freq = width // 8
     cols = freq // n_tm
@@ -84,7 +84,9 @@
     barrier = pltpu.get_barrier_semaphore()
     for chan, _, tm in group:
         pl.semaphore_signal(barrier, inc=1, device_id={"chan": chan, "tm": tm})
-    pl.semaphore_signal(barrier, inc=1, device_id={"chan": sibling, "tm": me})
+    across = z * 4 + (1 - hi) * 2 + 1 - core
+    for chan in (sibling, across):
+        pl.semaphore_signal(barrier, inc=1, device_id={"chan": chan, "tm": me})
     for d in range(1, n_z):
         pl.semaphore_signal(barrier, inc=1, device_id={"chan": above(d) * 4 + hi * 2 + core, "tm": me})
     load = pltpu.make_async_copy(table_ref.at[pl.ds(pl.multiple_of(core * freq, freq), freq)], table, table_sem.at[0])
@@ -95,7 +97,7 @@
     lags = raw.shape[2]
     for a in range(raw.shape[1]):
         x_ref[:, a * lags:(a + 1) * lags] = raw[:, a, :]
-    pl.semaphore_wait(barrier, len(group) + n_z)
+    pl.semaphore_wait(barrier, len(group) + n_z + 1)
 
     def remote(src, dst, send, recv, chan, tm):
         return pltpu.make_async_remote_copy(src_ref=src, dst_ref=dst, send_sem=send, recv_sem=recv,
@@ -106,8 +108,7 @@
         return remote(x_ref.at[pl.ds(pl.multiple_of((1 - core) * half, half), half), at], sib.at[:, at],
                       share_send.at[s], share_recv.at[s], sibling, me)
 
-    for s in range(2):
-        share(s).start()
+    share(0).start()
     blocks = [order_ref[k] for k in range(STEPS)]
     ahead = [lax.rem(z - blocks[k] // 4 + n_z, n_z) for k in range(STEPS)]
     own_core = [lax.rem(blocks[k], 2) == core for k in range(STEPS)]
@@ -128,6 +129,8 @@
         for k, s in subs:
             if t == 0 and k == 0 and s % (PARTS // 2) == 0:
                 share(s // (PARTS // 2)).wait()
+                if s == 0:
+                    share(1).start()
             for w in range(2):
                 if t >= reach[w][k]:
                     continue
@@ -296,19 +299,21 @@
         return remote(ref, ref, pass_send.at[slot], pass_recv.at[slot], sibling, me)
 
     def add_energy(d, energy):
-        pass_over(d, 1 - core).wait_recv()
         plane = above(d)
-        for k in range(STEPS):
-            for q in range(4):
-                r = k * SRC + q * 16
-                x = [pieces[q // 2, plane, k, n, (q % 2) * 16:(q % 2) * 16 + 16, :].astype(f32) for n in range(8)]
-                for n in range(8):
-                    s32[plane, n, r:r + 16, :] = x[n]
-
-                def out(n, value):
-                    fs[r:r + 16, n * 128:(n + 1) * 128] = value.astype(bf16)
-
-                features(x, out, False)
+        for c in (core, 1 - core):
+            if c is not core:
+                pass_over(d, 1 - core).wait_recv()
+            for k in range(STEPS):
+                for q in range(2):
+                    at = pl.ds(pl.multiple_of(k * SRC + c * half + q * 16, 16), 16)
+                    x = [pieces[c, plane, k, n, q * 16:q * 16 + 16, :].astype(f32) for n in range(8)]
+                    for n in range(8):
+                        s32[plane, n, at, :] = x[n]
+
+                    def out(n, value):
+                        fs[at, n * 128:(n + 1) * 128] = value.astype(bf16)
+
+                    features(x, out, False)
         return energy + lax.dot_general(fs[...], fr[plane], (((1,), (1,)), ((), ())), preferred_element_type=f32)
 
     for k, s in subs:
@@ -387,11 +392,13 @@
             def _():
                 act(to_owner(p, h))
 
+    def by_chip(value):
+        value = value.reshape(n_z, 2, 8, cols)
+        return [value[:, h].reshape(bins // 2, cols).astype(bf16) for h in range(2)]
+
     def hand_on(p):
         swap(p).wait_recv()
-        value = (mine[p] + got0[p].astype(f32)).reshape(n_z, 2, 8, cols)
-        for h in range(2):
-            out1[p, h] = value[:, h].reshape(bins // 2, cols).astype(bf16)
+        out1[p, 0], out1[p, 1] = by_chip(mine[p] + got0[p].astype(f32))
         to_owners(p, lambda copy: copy.start())
 
     def chunk(q):
@@ -415,7 +422,10 @@
         out = jnp.dot(place[...], jnp.concatenate(rows_of, 0).astype(bf16), preferred_element_type=f32)
         mine[p] = jnp.where(core == 0, out[:, :128], out[:, 128:])
         out0[p] = jnp.where(core == 0, out[:, 128:], out[:, :128]).astype(bf16)
-        swap(p).start()
+
+        @pl.when(q < n_tm - 1)
+        def _():
+            swap(p).start()
 
         @pl.when(q > 0)
         def _():
@@ -424,12 +434,24 @@
         return 0
 
     lax.fori_loop(0, n_tm, one_chunk, 0)
-    hand_on(me)
+    out1[me, 0], out1[me, 1] = by_chip(mine[me])
+    to_owners(me, lambda copy: copy.start())
+    last_out[0], last_out[1] = by_chip(out0[me].astype(f32))
+
+    def last(i, h, chan):
+        return remote(last_out.at[h], last_got.at[i], last_send.at[i], last_recv.at[i], chan, me)
+
+    lasts = [last(0, hi, sibling), last(1, 1 - hi, across)]
+    for copy in lasts[::-1]:
+        copy.start()
     total = out1[me, hi].astype(f32)
     for (chan, _, tm), (h, t) in zip(group, group_back):
         other = h * n_tm + t
         remote(out1.at[me, hi], got1.at[other], send4.at[me, hi], recv4.at[other], chan, tm).wait_recv()
         total = total + got1[other].astype(f32)
+    for i in range(2):
+        lasts[i].wait_recv()
+        total = total + last_got[i].astype(f32)
     out2[...] = total.reshape(out2.shape)
 
     def to_plane(d):
@@ -477,14 +499,18 @@
     for d in range(-far, far):
         pass_over(d, core).wait_send()
     for p in range(n_tm):
-        swap(p).wait_send()
         to_owners(p, lambda copy: copy.wait_send())
+
+        @pl.when(p != me)
+        def _():
+            swap(p).wait_send()
+
 
     for d in range(1, n_z):
         to_plane(d).wait_send()
     for i in range(2 * freq // lag):
         lag_swap(i).wait_send()
-    for copy in first + second + third + fifth:
+    for copy in first + second + third + fifth + lasts:
         copy.wait_send()
 
 
@@ -549,6 +575,8 @@
             vmem((n_tm, bins, cols), bf16),
             vmem((n_tm, 2, bins // 2, cols), bf16),
             vmem((2 * n_tm, bins // 2, cols), bf16),
+            vmem((2, bins // 2, cols), bf16),
+            vmem((2, bins // 2, cols), bf16),
             vmem((n_z, bins // n_z // 2, cols), f32),
             vmem((n_z, bins // n_z // 2, cols), f32),
             vmem((n_tm, bins // n_z // 2, cols), f32),
@@ -559,7 +587,7 @@
             dma((2, up, STEPS * PARTS)), dma((2, up, STEPS * PARTS)), dma((2,)), dma((2,)), dma((2 * n_tm,)), dma((2 * n_tm,)),
             dma((2, up, STEPS * PARTS)), dma((2, up, STEPS * PARTS)), dma((n_z,)), dma((n_z,)),
             dma((n_tm,)), dma((n_tm,)), dma((n_tm, 2)), dma((2 * n_tm,)), dma((n_z,)), dma((n_z,)),
-            dma((n_tm,)), dma((n_tm,)), dma((4,)), dma((4,)),
+            dma((2,)), dma((2,)), dma((n_tm,)), dma((n_tm,)), dma((4,)), dma((4,)),
         ],
         compiler_params=pltpu.CompilerParams(collective_id=0, has_side_effects=True, vmem_limit_bytes=58 * MIB),
         name="offset_stack",

time: 86.4 us -> 85.6 us (level)
  no operation moved by 1% of the time
where the time goes in v6:
time: 85.6 us; the launch traced here: 85.4 us
  Pallas kernels  84 us (98%)
  local copies, waits for them, and re-layouts  1.38 us (2%)
    pallas_call x1, Pallas kernels, local(): pl.pallas_call(functools.partial(kernel, n_chan, n_tm), out_shape=jax.Sha...  84 us

profile of v6, /device:TPU:1, one launch (start us, length us, event | category | flops | bytes accessed | tf_op | source)
XLA Modules:
  0.0 85.4 jit_solution(13880448170992079475)
XLA Ops:
  0.0 84.0 %offset_stack.1 = f32[4,2048]{1,0:T(4,128)} custom-call(s32[32]{0:T(128)} %order_ref.1, s32[16,128]{1,0:T(8,128)} %bitcast.1, bf16[64,4,2048]{2,1,0:T(4,128)(2,1)} %spectra_ref.1, bf16[2048,2048]{1,0:T(8,128)(2,1)} %constant.2.clone.table_ref), custom_call_target="tpu_custom_call" | custom-call | tf_op jit(solution)/shard_map/offset_stack/pallas_call | solution.py:540
  84.0 1.4 %copy.6 = f32[4,2048]{1,0:T(4,128)} copy(f32[4,2048]{1,0:T(4,128)} %offset_stack.1) | data formatting | bytes 65536

commit v7 on v6

--- a/solution.py
+++ b/solution.py
@@ -408,12 +408,15 @@
     project(0, chunk(0), wf0, t0)
     weigh(1)
 
-    def one_chunk(q, _):
+    def one_chunk(q, _, last_one=False):
         p = chunk(q)
         project(1, p, wf1, t1)
         gather(0, p, t0)
-        project(0, chunk(q + 1), wf0, t0)
+        if not last_one:
+            project(0, chunk(q + 1), wf0, t0)
         gather(1, p, t1)
+        if last_one:
+            hand_on(chunk(q - 1))
         rows_of = []
         for step in range(STEPS):
             value = jnp.sum(acc[step].reshape(span, 8, 256), axis=1)
@@ -422,10 +425,9 @@
         out = jnp.dot(place[...], jnp.concatenate(rows_of, 0).astype(bf16), preferred_element_type=f32)
         mine[p] = jnp.where(core == 0, out[:, :128], out[:, 128:])
         out0[p] = jnp.where(core == 0, out[:, 128:], out[:, :128]).astype(bf16)
-
-        @pl.when(q < n_tm - 1)
-        def _():
-            swap(p).start()
+        if last_one:
+            return 0
+        swap(p).start()
 
         @pl.when(q > 0)
         def _():
@@ -433,7 +435,8 @@
 
         return 0
 
-    lax.fori_loop(0, n_tm, one_chunk, 0)
+    lax.fori_loop(0, n_tm - 1, one_chunk, 0)
+    one_chunk(n_tm - 1, 0, True)
     out1[me, 0], out1[me, 1] = by_chip(mine[me])
     to_owners(me, lambda copy: copy.start())
     last_out[0], last_out[1] = by_chip(out0[me].astype(f32))

time: 85.6 us -> 85.7 us (level)
  no operation moved by 1% of the time
where the time goes in v7:
time: 85.7 us; the launch traced here: 85.4 us
  Pallas kernels  84 us (98%)
  local copies, waits for them, and re-layouts  1.38 us (2%)
    pallas_call x1, Pallas kernels, local(): pl.pallas_call(functools.partial(kernel, n_chan, n_tm), out_shape=jax.Sha...  84 us

profile of v7, /device:TPU:1, one launch (start us, length us, event | category | flops | bytes accessed | tf_op | source)
XLA Modules:
  0.0 85.4 jit_solution(8251393606853293519)
XLA Ops:
  0.0 84.0 %offset_stack.1 = f32[4,2048]{1,0:T(4,128)} custom-call(s32[32]{0:T(128)} %order_ref.1, s32[16,128]{1,0:T(8,128)} %bitcast.1, bf16[64,4,2048]{2,1,0:T(4,128)(2,1)} %spectra_ref.1, bf16[2048,2048]{1,0:T(8,128)(2,1)} %constant.2.clone.table_ref), custom_call_target="tpu_custom_call" | custom-call | tf_op jit(solution)/shard_map/offset_stack/pallas_call | solution.py:543
  84.1 1.4 %copy.6 = f32[4,2048]{1,0:T(4,128)} copy(f32[4,2048]{1,0:T(4,128)} %offset_stack.1) | data formatting | bytes 65536
